TPU v7x, 128 devices: a whole 4x4x4 slice. The times are simulated.
128 devices in a mesh: section: 4 (over x_lo, core), seq: 32 (over z, y, x_hi).
Axes of the slice: x: 4 (x_hi: 2, x_lo: 2; x = x_hi * 2 + x_lo), y: 4, z: 4, core: 2. Of those that a mesh axis runs over, the one named last changes fastest.
Arguments:
- saved_q: bfloat16 [4, 2, 2, 4096, 2048], P('section', None, None, 'seq'), may hold values from -6 to 6
- saved_k: bfloat16 [4, 2, 2, 4096, 2048], P('section', None, None, 'seq'), may hold values from -6 to 6
- saved_v: bfloat16 [4, 2, 2, 4096, 2048], P('section', None, None, 'seq'), may hold values from -6 to 6
- saved_o: bfloat16 [4, 2, 2, 4096, 2048], P('section', None, None, 'seq'), may hold values from -1.796875 to 1.796875
- saved_lse: float32 [4, 2, 2, 4096, 16], P('section', None, None, 'seq'), as said below
- cotangent: bfloat16 [4, 2, 4096, 3072], P('section', None, 'seq'), may hold values from -24 to 24
- out_weight: bfloat16 [4, 2048, 3072], P('section', 'seq'), may hold values from -0.125 to 0.125
- plan: int32 [4], P('section'), may hold values from 0 to 1
- control_map: int32 [5], replicated, may hold values from 0 to 3
- control_scale: float32 [5], replicated, may hold values from 0.25 to 1
Outputs:
- grad_q: bfloat16 [4, 2, 4096, 2048], P('section', None, 'seq')
- grad_k: bfloat16 [4, 2, 4096, 2048], P('section', None, 'seq')
- grad_v: bfloat16 [4, 2, 4096, 2048], P('section', None, 'seq')
- control_grad: bfloat16 [5, 2, 4096, 3072], P(None, None, 'seq', 'section')
Inputs may be any that keep to these rules, and one draw needn't show every extreme that they name: `saved_lse`: each value lies between the natural logarithm of 4096 and that plus one.
All inputs are finite; a program needn't handle non-finite values.
Results may differ from a plain program's by a relative error of at most 0.0061.
Values may be sent and summed in bfloat16 or wider, within the bound.
A program may use at most 128 MiB of HBM per device.

v0:
```python
import jax
import jax.numpy as jnp
from jax import lax
from jax.sharding import PartitionSpec as P


def spread(block, axis, owner):
    block = jnp.where(lax.axis_index(axis) == owner, block, jnp.zeros_like(block))
    return lax.psum(block, axis)


def to_heads(array, head_count):
    images, rows, width = array.shape
    head_size = width // head_count
    shaped = array.reshape(images, rows, head_count, head_size).transpose(0, 2, 1, 3)
    return shaped.reshape(images * head_count, rows, head_size)


def to_tokens(array, images):
    count, rows, head_size = array.shape
    head_count = count // images
    shaped = array.reshape(images, head_count, rows, head_size).transpose(0, 2, 1, 3)
    return shaped.reshape(images, rows, head_count * head_size)


def stat_heads(array):
    images, rows, head_count = array.shape
    return array.transpose(0, 2, 1).reshape(images * head_count, rows)


def attention_grads(query, keys, values, grads, lse, delta):
    count, total, head_size = query.shape
    scale = head_size ** (-0.5)
    block_rows = min(512, total)

    def block_step(carry, position):
        first_row = position * block_rows
        query_block = lax.dynamic_slice_in_dim(query, first_row, block_rows, 1)
        grads_block = lax.dynamic_slice_in_dim(grads, first_row, block_rows, 1)
        lse_block = lax.dynamic_slice_in_dim(lse, first_row, block_rows, 1)
        delta_block = lax.dynamic_slice_in_dim(delta, first_row, block_rows, 1)
        scores = (
            jnp.einsum("hrd,htd->hrt", query_block, keys, preferred_element_type=jnp.float32)
            * scale
        )
        probs = jnp.exp(scores - lse_block[:, :, None])
        grad_value = jnp.einsum(
            "hrt,hrd->htd",
            probs.astype(jnp.bfloat16),
            grads_block,
            preferred_element_type=jnp.float32,
        )
        grad_probs = jnp.einsum(
            "hrd,htd->hrt", grads_block, values, preferred_element_type=jnp.float32
        )
        grad_scores = (probs * (grad_probs - delta_block[:, :, None])).astype(jnp.bfloat16)
        grad_key = (
            jnp.einsum("hrt,hrd->htd", grad_scores, query_block, preferred_element_type=jnp.float32)
            * scale
        )
        grad_query = (
            jnp.einsum("hrt,htd->hrd", grad_scores, keys, preferred_element_type=jnp.float32)
            * scale
        )
        return ((carry[0] + grad_key, carry[1] + grad_value), grad_query.astype(jnp.bfloat16))

    zeros_sum = jnp.zeros((count, total, head_size), jnp.float32)
    positions = jnp.arange(total // block_rows, dtype=jnp.int32)
    (key_sum, value_sum), query_blocks = lax.scan(block_step, (zeros_sum, zeros_sum), positions)
    grad_query = query_blocks.transpose(1, 0, 2, 3).reshape(count, total, head_size)
    return (grad_query, key_sum.astype(jnp.bfloat16), value_sum.astype(jnp.bfloat16))


def shards(
    saved_q,
    saved_k,
    saved_v,
    saved_o,
    saved_lse,
    cotangent,
    out_weight,
    plan,
    control_map,
    control_scale,
):
    picked = plan[0]

    def select(array):
        return lax.dynamic_index_in_dim(array[0], picked, 0, keepdims=False)

    query_rows = select(saved_q)
    key_rows = select(saved_k)
    value_rows = select(saved_v)
    output_rows = select(saved_o)
    lse_rows = select(saved_lse)
    grad_out = cotangent[0]
    images, local_rows, width = query_rows.shape
    head_count = lse_rows.shape[2]
    flat_out = grad_out.reshape(images * local_rows, grad_out.shape[2])
    grad_attn = jnp.einsum(
        "td,wd->tw",
        flat_out,
        lax.all_gather(out_weight[0], "seq", axis=0, tiled=True),
        preferred_element_type=jnp.float32,
    )
    grad_attn = grad_attn.astype(jnp.bfloat16).reshape(images, local_rows, width)
    lse_heads = stat_heads(lse_rows)
    query_h, key_h, value_h, grads_h, output_h = (
        lax.all_to_all(
            to_heads(query_rows, head_count), "seq", split_axis=0, concat_axis=1, tiled=True
        ),
        lax.all_to_all(
            to_heads(key_rows, head_count), "seq", split_axis=0, concat_axis=1, tiled=True
        ),
        lax.all_to_all(
            to_heads(value_rows, head_count), "seq", split_axis=0, concat_axis=1, tiled=True
        ),
        lax.all_to_all(
            to_heads(grad_attn, head_count), "seq", split_axis=0, concat_axis=1, tiled=True
        ),
        lax.all_to_all(
            to_heads(output_rows, head_count), "seq", split_axis=0, concat_axis=1, tiled=True
        ),
    )
    lse_all = lax.all_to_all(lse_heads, "seq", split_axis=0, concat_axis=1, tiled=True)
    delta_all = jnp.sum(grads_h.astype(jnp.float32) * output_h.astype(jnp.float32), axis=2)
    query_grad_h, key_grad_h, value_grad_h = attention_grads(
        query_h, key_h, value_h, grads_h, lse_all, delta_all
    )
    query_back, key_back, value_back = (
        lax.all_to_all(query_grad_h, "seq", split_axis=1, concat_axis=0, tiled=True),
        lax.all_to_all(key_grad_h, "seq", split_axis=1, concat_axis=0, tiled=True),
        lax.all_to_all(value_grad_h, "seq", split_axis=1, concat_axis=0, tiled=True),
    )
    grad_query = to_tokens(query_back, images)
    grad_key = to_tokens(key_back, images)
    grad_value = to_tokens(value_back, images)
    channels = grad_out.shape[2] // lax.axis_size("section")
    position = lax.axis_index("section")
    matched_list = []
    for block_index in range(control_map.shape[0]):
        matched = spread(grad_out, "section", control_map[block_index])
        matched_list.append(lax.dynamic_slice_in_dim(matched, position * channels, channels, 2))
    matched_all = jnp.stack(matched_list).astype(jnp.float32)
    control_grad = (control_scale[:, None, None, None] * matched_all).astype(jnp.bfloat16)
    return (grad_query[None], grad_key[None], grad_value[None], control_grad)


def solution(mesh):
    placed = (
        P("section", None, None, "seq", None),
        P("section", None, None, "seq", None),
        P("section", None, None, "seq", None),
        P("section", None, None, "seq", None),
        P("section", None, None, "seq", None),
        P("section", None, "seq", None),
        P("section", "seq", None),
        P("section"),
        P(),
        P(),
    )
    return jax.shard_map(
        shards,
        mesh=mesh,
        in_specs=placed,
        out_specs=(
            P("section", None, "seq", None),
            P("section", None, "seq", None),
            P("section", None, "seq", None),
            P(None, None, "seq", "section"),
        ),
        check_vma=False,
    )
```

profile of v0, /device:TPU:0, one launch (start us, length us, event | category | flops | bytes accessed | tf_op | source)
XLA Modules:
  0.0 532.0 jit_solution(15327912376544809501)
XLA Ops:
  12.4 10.9 %all-to-all-start.1 = ((bf16[32,128,128]{1,2,0:T(8,128)(2,1)}), bf16[32,128,128]{1,2,0:T(8,128)(2,1)S(1)}, u32[]{:S(2)}, u32[]{:S(2)}) async-start(bf16[32,128,128]{1,2,0:T(8,128)(2,1)} %bitcast.179), calls=%async_computation.1 | async-start | bytes 2097152 | tf_op jit(solution)/shard_map/all_to_all | solution.py:112
  24.6 21.0 %all-to-all-done.1 = bf16[32,128,128]{1,2,0:T(8,128)(2,1)S(1)} async-done(((bf16[32,128,128]{1,2,0:T(8,128)(2,1)}), bf16[32,128,128]{1,2,0:T(8,128)(2,1)S(1)}, u32[]{:S(2)}, u32[]{:S(2)}) %all-to-all-start.1) | async-done | bytes 1048608 | tf_op jit(solution)/shard_map/all_to_all | solution.py:112
  45.5 4.7 all-to-all-start
  53.2 2.4 copy.77
  55.6 21.8 %all-to-all-done = bf16[32,128,128]{1,2,0:T(8,128)(2,1)} async-done(((bf16[32,128,128]{1,2,0:T(8,128)(2,1)}), bf16[32,128,128]{1,2,0:T(8,128)(2,1)}, u32[]{:S(2)}, u32[]{:S(2)}) %all-to-all-start) | async-done | bytes 1048608 | tf_op jit(solution)/shard_map/all_to_all | solution.py:109
  77.4 3.9 all-to-all-start.5
  86.4 10.1 %all-to-all-done.5 = bf16[32,128,128]{2,1,0:T(8,128)(2,1)S(1)} async-done(((bf16[32,128,128]{2,1,0:T(8,128)(2,1)}), bf16[32,128,128]{2,1,0:T(8,128)(2,1)S(1)}, u32[]{:S(2)}, u32[]{:S(2)}) %all-to-all-start.5) | async-done | bytes 1048608 | tf_op jit(solution)/shard_map/all_to_all | solution.py:121
  96.5 4.3 all-to-all-start.4
  100.9 73.0 %all-gather.3.cloned.1.call-done = bf16[1,2048,3072]{2,1,0:T(8,128)(2,1)} async-done(((bf16[1,64,3072]{2,1,0:T(8,128)(2,1)}), bf16[1,2048,3072]{2,1,0:T(8,128)(2,1)}) %all-gather.3.cloned.1.call-update) | async-done | bytes 12582928 | tf_op jit(solution)/shard_map/all_gather | solution.py:103
  173.9 8.5 %fusion.32 = bf16[32,8,16,128]{3,1,2,0:T(8,128)(2,1)S(1)} fusion(bf16[256,3072]{1,0:T(8,128)(2,1)} %bitcast.185, bf16[1,2048,3072]{2,1,0:T(8,128)(2,1)} %all-gather.3.cloned.1.call-done), kind=kOutput, calls=%fused_computation.43 | convolution fusion | flops 3221749760 | bytes 15204352 | tf_op jit(solution)/shard_map/td,wd->tw/dot_general | solution.py:100
  183.9 5.9 %all-to-all-start.3 = ((bf16[32,128,128]{2,1,0:T(8,128)(2,1)}), bf16[32,128,128]{2,1,0:T(8,128)(2,1)}, u32[]{:S(2)}, u32[]{:S(2)}) async-start(bf16[32,128,128]{2,1,0:T(8,128)(2,1)} %bitcast.16), calls=%async_computation.3 | async-start | bytes 2097152 | tf_op jit(solution)/shard_map/all_to_all | solution.py:118
  189.8 4.7 select_bitcast_fusion
  196.5 2.3 copy.70
  200.4 8.3 %all-to-all-done.3 = bf16[32,128,128]{2,1,0:T(8,128)(2,1)} async-done(((bf16[32,128,128]{2,1,0:T(8,128)(2,1)}), bf16[32,128,128]{2,1,0:T(8,128)(2,1)}, u32[]{:S(2)}, u32[]{:S(2)}) %all-to-all-start.3) | async-done | bytes 1048608 | tf_op jit(solution)/shard_map/all_to_all | solution.py:118
  208.7 4.3 all-to-all-start.2
  213.0 2.3 multiply_reduce_fusion
  215.3 7.5 %all-to-all-done.2 = f32[32,1,128]{2,1,0:T(1,128)S(1)} async-done(((f32[32,1,128]{2,1,0:T(1,128)}), f32[32,1,128]{2,1,0:T(1,128)S(1)}, u32[]{:S(2)}, u32[]{:S(2)}) %all-to-all-start.2) | async-done | bytes 16416 | tf_op jit(solution)/shard_map/all_to_all | solution.py:125
  222.7 136.9 %while.15 = (s32[]{:T(128)}, f32[1,4096,128]{2,1,0:T(8,128)}, f32[1,4096,128]{2,1,0:T(8,128)S(1)}, bf16[8,1,512,128]{3,2,1,0:T(8,128)(2,1)}, s32[8]{0:T(128)S(1)...) while((s32[]{:T(128)}, f32[1,4096,128]{2,1,0:T(8,128)}, ...), condition=%wide.region_2.3_spmd.clone, body=%wide.region_1.2_spmd.clone.sunk | while | flops 2703884288 | bytes 70924608 | solution.py:69
  224.0 2.6 fusion.63
  226.6 3.5 fusion.65
  230.2 3.3 multiply_convert_fusion.3
  235.4 3.1 fusion.64
  241.1 2.6 fusion.63
  243.7 3.5 fusion.65
  247.3 3.3 multiply_convert_fusion.3
  252.5 3.1 fusion.64
  258.2 2.6 fusion.63
  260.8 3.5 fusion.65
  264.3 3.3 multiply_convert_fusion.3
  269.6 3.1 fusion.64
  275.3 2.6 fusion.63
  277.9 3.5 fusion.65
  281.4 3.4 multiply_convert_fusion.3
  286.7 3.1 fusion.64
  292.4 2.6 fusion.63
  295.0 3.5 fusion.65
  298.6 3.3 multiply_convert_fusion.3
  303.8 3.1 fusion.64
  309.5 2.6 fusion.63
  312.1 3.5 fusion.65
  315.7 3.3 multiply_convert_fusion.3
  319.0 1.9 fusion.66
  320.9 3.1 fusion.64
  326.6 2.6 fusion.63
  329.2 3.5 fusion.65
  332.8 3.3 multiply_convert_fusion.3
  338.0 3.1 fusion.64
  343.8 2.6 fusion.63
  346.3 3.5 fusion.65
  349.9 3.3 multiply_convert_fusion.3
  355.1 3.1 fusion.64
  359.6 4.3 copy.100
  364.5 23.5 %reduce.1 = bf16[4096,128]{1,0:T(8,128)(2,1)S(1)} reduce(bf16[4096,1,128]{2,1,0:T(2,128)(2,1)} %bitcast.170, bf16[]{:T(256)} %broadcast.64), dimensions={1}, to_apply=%bitcast.131.reduce_sub_computation | reduce | bytes 2097154
  389.1 4.1 all-to-all-start.6
  394.9 17.0 %copy.99 = bf16[1,4096,128]{2,0,1:T(2,128)(2,1)} copy(bf16[1,4096,128]{2,1,0:T(8,128)(2,1)S(1)} %convert_element_type.42) | data formatting | bytes 2097152 | tf_op jit(solution)/shard_map/convert_element_type | solution.py:71
  411.9 24.4 %reduce.2 = bf16[4096,128]{1,0:T(8,128)(2,1)} reduce(bf16[4096,1,128]{2,1,0:T(2,128)(2,1)} %bitcast.172, bf16[]{:T(256)} %broadcast.64), dimensions={1}, to_apply=%bitcast.130.reduce_sub_computation | reduce | bytes 2097154
  436.4 2.1 reshape.182
  438.5 10.2 %all-to-all-start.7 = ((bf16[32,2,8192]{2,1,0:T(2,128)(2,1)}), bf16[32,2,8192]{2,1,0:T(2,128)(2,1)}, u32[]{:S(2)}, u32[]{:S(2)}) async-start(bf16[32,2,8192]{2,1,0:T(2,128)(2,1)} %reshape.182), calls=%async_computation.7 | async-start | bytes 2097152 | tf_op jit(solution)/shard_map/all_to_all | solution.py:132
  448.9 16.7 %copy.98 = bf16[1,4096,128]{2,0,1:T(2,128)(2,1)S(1)} copy(bf16[1,4096,128]{2,1,0:T(8,128)(2,1)S(1)} %convert_element_type.43) | data formatting | bytes 2097152 | tf_op jit(solution)/shard_map/convert_element_type | solution.py:71
  465.6 23.4 %reduce.3 = bf16[4096,128]{1,0:T(8,128)(2,1)} reduce(bf16[4096,1,128]{2,1,0:T(2,128)(2,1)S(1)} %bitcast.171, bf16[]{:T(256)} %broadcast.64), dimensions={1}, to_apply=%bitcast.129.reduce_sub_computation | reduce | bytes 2097154
  489.0 2.1 reshape.184
  491.2 10.0 %all-to-all-start.8 = ((bf16[32,2,8192]{2,1,0:T(2,128)(2,1)}), bf16[32,2,8192]{2,1,0:T(2,128)(2,1)}, u32[]{:S(2)}, u32[]{:S(2)}) async-start(bf16[32,2,8192]{2,1,0:T(2,128)(2,1)} %reshape.184), calls=%async_computation.8 | async-start | bytes 2097152 | tf_op jit(solution)/shard_map/all_to_all | solution.py:133
  511.4 4.3 reshape.183
  517.9 4.3 reshape.185
  (128 shorter events, 61.8 us)
Async XLA Ops:
  8.0 186.6 %copy-start = (f32[1,2,2,128,16]{3,4,2,1,0:T(8,128)S(1)}, f32[1,2,2,128,16]{3,4,2,1,0:T(8,128)}, u32[]{:S(2)}) copy-start(f32[1,2,2,128,16]{3,4,2,1,0:T(8,128)} %param.16) | copy-start | bytes 98308
  8.0 165.9 %all-gather.3.cloned.1.call-start = ((), (), s32[]{:S(2)}) async-start(), calls=%async_computation.9 | async-start | bytes 12976128 | tf_op jit(solution)/shard_map/all_gather | solution.py:103
  12.4 33.2 %all-to-all-start.1 = ((bf16[32,128,128]{1,2,0:T(8,128)(2,1)}), bf16[32,128,128]{1,2,0:T(8,128)(2,1)S(1)}, u32[]{:S(2)}, u32[]{:S(2)}) async-start(bf16[32,128,128]{1,2,0:T(8,128)(2,1)} %bitcast.179), calls=%async_computation.1 | async-start | bytes 2097152 | tf_op jit(solution)/shard_map/all_to_all | solution.py:112
  45.5 31.9 %all-to-all-start = ((bf16[32,128,128]{1,2,0:T(8,128)(2,1)}), bf16[32,128,128]{1,2,0:T(8,128)(2,1)}, u32[]{:S(2)}, u32[]{:S(2)}) async-start(bf16[32,128,128]{1,2,0:T(8,128)(2,1)} %bitcast.3), calls=%async_computation | async-start | bytes 2097152 | tf_op jit(solution)/shard_map/all_to_all | solution.py:109
  53.2 28.1 %copy-start.7 = (s32[5]{0:T(128)S(1)}, s32[5]{0:T(128)}, u32[]{:S(2)}) copy-start(s32[5]{0:T(128)} %param.20) | copy-start | bytes 64
  77.4 19.1 %all-to-all-start.5 = ((bf16[32,128,128]{2,1,0:T(8,128)(2,1)}), bf16[32,128,128]{2,1,0:T(8,128)(2,1)S(1)}, u32[]{:S(2)}, u32[]{:S(2)}) async-start(bf16[32,128,128]{2,1,0:T(8,128)(2,1)} %bitcast.177), calls=%async_computation.5 | async-start | bytes 2097152 | tf_op jit(solution)/shard_map/all_to_all | solution.py:121
  96.5 85.9 %copy-start.5 = (bf16[32,128,128]{2,1,0:T(8,128)(2,1)}, bf16[32,128,128]{2,1,0:T(8,128)(2,1)S(1)}, u32[]{:S(2)}) copy-start(bf16[32,128,128]{2,1,0:T(8,128)(2,1)S(1)} %all-to-all-done.5) | copy-start | bytes 3145732
  96.5 87.3 %all-to-all-start.4 = ((bf16[32,128,128]{1,2,0:T(8,128)(2,1)}), bf16[32,128,128]{1,2,0:T(8,128)(2,1)S(1)}, u32[]{:S(2)}, u32[]{:S(2)}) async-start(bf16[32,128,128]{1,2,0:T(8,128)(2,1)} %bitcast.178), calls=%async_computation.4 | async-start | bytes 2097152 | tf_op jit(solution)/shard_map/all_to_all | solution.py:115
  183.9 10.7 %copy-start.6 = (bf16[32,128,128]{1,2,0:T(8,128)(2,1)}, bf16[32,128,128]{1,2,0:T(8,128)(2,1)S(1)}, u32[]{:S(2)}) copy-start(bf16[32,128,128]{1,2,0:T(8,128)(2,1)S(1)} %all-to-all-done.4) | copy-start | bytes 3145732
  183.9 24.8 %all-to-all-start.3 = ((bf16[32,128,128]{2,1,0:T(8,128)(2,1)}), bf16[32,128,128]{2,1,0:T(8,128)(2,1)}, u32[]{:S(2)}, u32[]{:S(2)}) async-start(bf16[32,128,128]{2,1,0:T(8,128)(2,1)} %bitcast.16), calls=%async_computation.3 | async-start | bytes 2097152 | tf_op jit(solution)/shard_map/all_to_all | solution.py:118
  189.8 311.5 %all-reduce.3.cloned.1.call-start = ((), (), s32[]{:S(2)}) async-start(), calls=%async_computation.10 | async-start | bytes 15728640 | tf_op jit(solution)/shard_map/psum | solution.py:9
  208.7 14.0 %all-to-all-start.2 = ((f32[32,1,128]{2,1,0:T(1,128)}), f32[32,1,128]{2,1,0:T(1,128)S(1)}, u32[]{:S(2)}, u32[]{:S(2)}) async-start(f32[32,1,128]{2,1,0:T(1,128)} %bitcast.11), calls=%async_computation.2 | async-start | bytes 32768 | tf_op jit(solution)/shard_map/all_to_all | solution.py:125
  230.2 3.3 copy-start.4
  233.5 1.9 copy-start.2
  238.6 1.3 copy-start.3
  247.2 3.3 copy-start.4
  250.6 1.9 copy-start.2
  255.6 1.3 copy-start.3
  264.3 3.3 copy-start.4
  267.7 1.9 copy-start.2
  272.7 1.3 copy-start.3
  281.4 3.4 copy-start.4
  284.8 1.9 copy-start.2
  289.9 1.3 copy-start.3
  298.6 3.3 copy-start.4
  301.9 1.9 copy-start.2
  307.0 1.3 copy-start.3
  315.6 3.3 copy-start.4
  319.0 1.9 copy-start.2
  324.0 1.3 copy-start.3
  332.8 3.3 copy-start.4
  336.1 1.9 copy-start.2
  341.2 1.3 copy-start.3
  349.9 3.3 copy-start.4
  353.2 1.9 copy-start.2
  358.3 1.3 copy-start.3
  389.1 49.4 %all-to-all-start.6 = ((bf16[32,2,8192]{2,1,0:T(2,128)(2,1)}), bf16[32,2,8192]{2,1,0:T(2,128)(2,1)S(1)}, u32[]{:S(2)}, u32[]{:S(2)}) async-start(bf16[32,2,8192]{2,1,0:T(2,128)(2,1)} %reshape.180), calls=%async_computation.6 | async-start | bytes 2097152 | tf_op jit(solution)/shard_map/all_to_all | solution.py:131
  438.5 52.7 %all-to-all-start.7 = ((bf16[32,2,8192]{2,1,0:T(2,128)(2,1)}), bf16[32,2,8192]{2,1,0:T(2,128)(2,1)}, u32[]{:S(2)}, u32[]{:S(2)}) async-start(bf16[32,2,8192]{2,1,0:T(2,128)(2,1)} %reshape.182), calls=%async_computation.7 | async-start | bytes 2097152 | tf_op jit(solution)/shard_map/all_to_all | solution.py:132
  491.2 26.7 %all-to-all-start.8 = ((bf16[32,2,8192]{2,1,0:T(2,128)(2,1)}), bf16[32,2,8192]{2,1,0:T(2,128)(2,1)}, u32[]{:S(2)}, u32[]{:S(2)}) async-start(bf16[32,2,8192]{2,1,0:T(2,128)(2,1)} %reshape.184), calls=%async_computation.8 | async-start | bytes 2097152 | tf_op jit(solution)/shard_map/all_to_all | solution.py:133
  501.2 5.2 copy-start.8
  522.3 2.0 copy-start.1
Sparse Core Ops, SparseCore 0:
  11.8 161.9 all-gather.2
Sparse Core Ops, SparseCore 1:
  194.7 153.3 all-reduce.2
where the time goes:
time: 543 us; the launch traced here: 532 us
  waiting for transfers between devices  142 us (26%)
  matrix products  124 us (23%)
  local copies, waits for them, and re-layouts  99.6 us (18%)
  other arithmetic  82 us (15%)
  starting transfers between devices  58.5 us (11%)
  between operations  19.8 us (4%)
  loops' own time  5.63 us (1%)
    all_gather x1, waiting for transfers between devices, shards(): lax.all_gather(out_weight[0], 'seq', axis=0, tiled=True)  73 us
    unnamed x5, other arithmetic  71.3 us
    unnamed x34, local copies, waits for them, and re-layouts  29.6 us
    dot_general x8, matrix products, block_step(): jnp.einsum('hrt,hrd->htd', probs.astype(jnp.bfloat16), grads_block, prefe...  28.3 us
    dot_general x8, matrix products, block_step(): jnp.einsum('hrd,htd->hrt', grads_block, values, preferred_element_type=jn...  26.5 us
    dot_general x8, matrix products, block_step(): jnp.einsum('hrt,hrd->htd', grad_scores, query_block, preferred_element_ty...  25 us
    all_to_all x1, waiting for transfers between devices, shards(): lax.all_to_all(to_heads(query_rows, head_count), 'seq', split_axis=0, con...  21.8 us
    all_to_all x1, waiting for transfers between devices, shards(): lax.all_to_all(to_heads(key_rows, head_count), 'seq', split_axis=0, conca...  21 us
  transfers between devices with their start and end apart: 11, of which 6 were waited for; matrix products, arithmetic and copies ran while one was open for 54% of the time, Pallas kernels for 0%

commit v1 on v0

v1 whole, which is shorter than its diff:
```python
import functools
import math

import jax
import jax.numpy as jnp
from jax import lax
from jax.experimental import pallas as pl
from jax.experimental.pallas import tpu as pltpu
from jax.sharding import PartitionSpec as P

F32 = jnp.float32
BF16 = jnp.bfloat16
NT = (((1,), (1,)), ((), ()))
NN = (((1,), (0,)), ((), ()))


def dot(a, b, dims):
    return lax.dot_general(a, b, dims, preferred_element_type=F32)


def attention_kernel(block_keys, block_queries, unroll, q, k, v, g, stats, dq, dk, dv, dq_sum):
    total, head_size = q.shape
    scale = head_size**-0.5
    scale2 = scale * math.log2(math.e)
    dq_sum[...] = jnp.zeros_like(dq_sum)

    @pl.loop(0, total // block_keys)
    def _(u):
        us = pl.ds(pl.multiple_of(u * block_keys, block_keys), block_keys)
        kb, vb = k[us, :], v[us, :]
        kt = kb.T

        def inner(t, carry):
            sum_k, sum_v = carry
            ts = pl.ds(pl.multiple_of(t * block_queries, block_queries), block_queries)
            qb, gb = q[ts, :], g[ts, :]
            p = jnp.exp2(dot(kb, qb, NT) * scale2 - stats[0:1, ts])
            sum_v = sum_v + dot(p.astype(BF16), gb, NN)
            ds = (p * (dot(vb, gb, NT) - stats[1:2, ts])).astype(BF16)
            sum_k = sum_k + dot(ds, qb, NN)
            dq_sum[:, ts] += dot(kt, ds, NN)
            return sum_k, sum_v

        zeros = jnp.zeros((block_keys, head_size), F32)
        sum_k, sum_v = lax.fori_loop(0, total // block_queries, inner, (zeros, zeros), unroll=unroll)
        dk[us, :] = (sum_k * scale).astype(BF16)
        dv[us, :] = sum_v.astype(BF16)

    dq[...] = (dq_sum[...] * scale).astype(BF16).T


def attention_grads(q, k, v, g, stats):
    total, head_size = q.shape
    out = jax.ShapeDtypeStruct((total, head_size), BF16)
    whole = pl.BlockSpec(memory_space=pltpu.VMEM)
    return pl.pallas_call(
        functools.partial(attention_kernel, 1024, 512, 4),
        out_shape=(out, out, out),
        in_specs=[whole] * 5,
        out_specs=(whole, whole, whole),
        scratch_shapes=[pltpu.VMEM((head_size, total), F32)],
        compiler_params=pltpu.CompilerParams(vmem_limit_bytes=56 * 2**20),
        cost_estimate=pl.CostEstimate(
            flops=10 * total * total * head_size, bytes_accessed=16 * total * head_size, transcendentals=0
        ),
        name="attention_grads",
    )(q, k, v, g, stats)


def to_heads(array, head_count):
    images, rows, width = array.shape
    head_size = width // head_count
    shaped = array.reshape(images, rows, head_count, head_size).transpose(0, 2, 1, 3)
    return shaped.reshape(images * head_count, rows, head_size)


def to_tokens(array, images):
    count, rows, head_size = array.shape
    head_count = count // images
    shaped = array.reshape(images, head_count, rows, head_size).transpose(0, 2, 1, 3)
    return shaped.reshape(images, rows, head_count * head_size)


def shards(
    saved_q,
    saved_k,
    saved_v,
    saved_o,
    saved_lse,
    cotangent,
    out_weight,
    plan,
    control_map,
    control_scale,
):
    picked = plan[0]

    def select(array):
        return lax.dynamic_index_in_dim(array[0], picked, 0, keepdims=False)

    def exchange(array):
        return lax.all_to_all(array, "seq", split_axis=0, concat_axis=0, tiled=True)

    lse_rows = select(saved_lse)
    output_rows = select(saved_o)
    grad_out = cotangent[0]
    images, local_rows, depth = grad_out.shape
    head_count = lse_rows.shape[2]
    width = output_rows.shape[2]
    head_size = width // head_count
    weight = lax.all_gather(out_weight[0], "seq", axis=0, tiled=True)
    grad_attn = dot(grad_out.reshape(images * local_rows, depth), weight, NT)
    grad_attn = grad_attn.astype(BF16).reshape(images, local_rows, width)
    products = grad_attn.astype(F32) * output_rows.astype(F32)
    delta = jnp.sum(products.reshape(images, local_rows, head_count, head_size), axis=3)
    stats = jnp.stack([lse_rows * math.log2(math.e), delta], axis=3)
    stats = stats.transpose(0, 2, 3, 1).reshape(images * head_count, 2, local_rows)
    q, k, v, g = (
        exchange(to_heads(rows, head_count)).reshape(-1, head_size)
        for rows in (select(saved_q), select(saved_k), select(saved_v), grad_attn)
    )
    stats = exchange(stats).transpose(1, 0, 2).reshape(2, -1)
    grads = attention_grads(q, k, v, g, stats)
    backs = tuple(
        to_tokens(exchange(grad.reshape(-1, local_rows, head_size)), images)[None] for grad in grads
    )
    sections = lax.axis_size("section")
    pieces = grad_out.reshape(images, local_rows, sections, depth // sections).transpose(2, 0, 1, 3)
    pieces = lax.all_to_all(pieces, "section", split_axis=0, concat_axis=0, tiled=True)
    matched = jnp.take(pieces, control_map, axis=0, mode="clip").astype(F32)
    control_grad = (control_scale[:, None, None, None] * matched).astype(BF16)
    return (*backs, control_grad)


def solution(mesh):
    placed = (
        P("section", None, None, "seq", None),
        P("section", None, None, "seq", None),
        P("section", None, None, "seq", None),
        P("section", None, None, "seq", None),
        P("section", None, None, "seq", None),
        P("section", None, "seq", None),
        P("section", "seq", None),
        P("section"),
        P(),
        P(),
    )
    return jax.shard_map(
        shards,
        mesh=mesh,
        in_specs=placed,
        out_specs=(
            P("section", None, "seq", None),
            P("section", None, "seq", None),
            P("section", None, "seq", None),
            P(None, None, "seq", "section"),
        ),
        check_vma=False,
    )
```

time: 543 us -> 347 us (0.64); the launches traced: 532 us -> 345 us
  matrix products: 124 us -> 8.5 us
  other arithmetic: 82 us -> 6.61 us
  local copies, waits for them, and re-layouts: 99.6 us -> 25.8 us
  blocking collectives: 0 us -> 47.6 us
  Pallas kernels: 0 us -> 47.2 us
  starting transfers between devices: 58.5 us -> 38.3 us
  waiting for transfers between devices: 142 us -> 157 us
  loops' own time: 5.63 us -> 0 us
    dot_general x41 -> x1, matrix products: 124 us -> 8.5 us  [dot(): return lax.dot_general(a, b, dims, preferred_element_type=F32)]
    unnamed x5 -> x0, other arithmetic: 71.3 us -> none
    all_to_all x0 -> x2, blocking collectives: none -> 47.6 us  [exchange(): return lax.all_to_all(array, 'seq', split_axis=0, concat_axis=0, tiled=True)]
    pallas_call x0 -> x1, Pallas kernels: none -> 47.2 us  [attention_grads(): pl.pallas_call(functools.partial(attention_kernel, 1024, 512, 4), out_sha...]
    convert_element_type x2 -> x0, local copies, waits for them, and re-layouts: 33.8 us -> none  [the longest x1 17 us: attention_grads(): key_sum.astype(jnp.bfloat16)]
    unnamed x34 -> x27, local copies, waits for them, and re-layouts: 29.6 us -> 4.72 us
    all_to_all x9 -> x7, starting transfers between devices: 58.4 us -> 38.3 us  [the longest x6 34.6 us: exchange(): return lax.all_to_all(array, 'seq', split_axis=0, concat_axis=0, tiled=True)]
    all_gather x1, waiting for transfers between devices: 73 us -> 86.3 us  [shards(): weight = lax.all_gather(out_weight[0], 'seq', axis=0, tiled=True)]
  transfers between devices with their start and end apart: 11 -> 8, of which waited for: 6 -> 6; matrix products, arithmetic and copies ran while one was open for 54% -> 11% of each run, Pallas kernels for 0% -> 14%
where the time goes in v1:
time: 347 us; the launch traced here: 345 us
  waiting for transfers between devices  157 us (45%)
  blocking collectives  47.6 us (14%)
  Pallas kernels  47.2 us (14%)
  starting transfers between devices  38.3 us (11%)
  local copies, waits for them, and re-layouts  25.8 us (7%)
  between operations  14.9 us (4%)
  matrix products  8.5 us (2%)
  other arithmetic  6.61 us (2%)
    all_gather x1, waiting for transfers between devices, shards(): weight = lax.all_gather(out_weight[0], 'seq', axis=0, tiled=True)  86.3 us
    all_to_all x6, waiting for transfers between devices, exchange(): return lax.all_to_all(array, 'seq', split_axis=0, concat_axis=0, tiled=True)  69.6 us
    all_to_all x2, blocking collectives, exchange(): return lax.all_to_all(array, 'seq', split_axis=0, concat_axis=0, tiled=True)  47.6 us
    pallas_call x1, Pallas kernels, attention_grads(): pl.pallas_call(functools.partial(attention_kernel, 1024, 512, 4), out_sha...  47.2 us
    all_to_all x6, starting transfers between devices, exchange(): return lax.all_to_all(array, 'seq', split_axis=0, concat_axis=0, tiled=True)  34.6 us
    dot_general x1, matrix products, dot(): return lax.dot_general(a, b, dims, preferred_element_type=F32)  8.5 us
  transfers between devices with their start and end apart: 8, of which 6 were waited for; matrix products, arithmetic and copies ran while one was open for 11% of the time, Pallas kernels for 14%

profile of v1, /device:TPU:0, one launch (start us, length us, event | category | flops | bytes accessed | tf_op | source)
XLA Modules:
  0.0 345.5 jit_solution(3185303232427389963)
XLA Ops:
  7.2 0.0 copy-start
  7.2 0.0 all-gather.3.cloned.1.call-start
  7.2 0.7 all-gather.3.cloned.1.call-update
  8.6 1.7 constant_dynamic-slice_fusion.2
  10.2 0.7 copy.98
  10.9 1.3 copy.85
  12.2 10.9 %all-to-all-start.1 = ((bf16[32,128,128]{2,1,0:T(8,128)(2,1)}), bf16[32,128,128]{2,1,0:T(8,128)(2,1)S(1)}, u32[]{:S(2)}, u32[]{:S(2)}) async-start(bf16[32,128,128]{2,1,0:T(8,128)(2,1)} %copy.85), calls=%async_computation.1 | async-start | bytes 2097152 | tf_op jit(solution)/shard_map/all_to_all | solution.py:102
  23.1 0.7 copy.97
  23.8 1.3 copy.83
  25.1 0.0 copy-start.6
  25.1 20.2 %all-to-all-done.1 = bf16[32,128,128]{2,1,0:T(8,128)(2,1)S(1)} async-done(((bf16[32,128,128]{2,1,0:T(8,128)(2,1)}), bf16[32,128,128]{2,1,0:T(8,128)(2,1)S(1)}, u32[]{:S(2)}, u32[]{:S(2)}) %all-to-all-start.1) | async-done | bytes 1048608 | tf_op jit(solution)/shard_map/all_to_all | solution.py:102
  45.3 0.0 copy-start.4
  45.3 4.7 %all-to-all-start = ((bf16[32,128,128]{2,1,0:T(8,128)(2,1)}), bf16[32,128,128]{2,1,0:T(8,128)(2,1)}, u32[]{:S(2)}, u32[]{:S(2)}) async-start(bf16[32,128,128]{2,1,0:T(8,128)(2,1)} %copy.83), calls=%async_computation | async-start | bytes 2097152 | tf_op jit(solution)/shard_map/all_to_all | solution.py:102
  50.0 0.0 copy-done
  50.0 0.1 copy.100
  50.1 0.0 copy-done.6
  50.1 2.5 dynamic-slice_convert_fusion
  52.6 0.0 copy-done.4
  52.6 0.4 copy.102
  53.0 1.7 copy.99
  54.8 1.3 copy.87
  56.1 21.1 %all-to-all-done = bf16[32,128,128]{2,1,0:T(8,128)(2,1)} async-done(((bf16[32,128,128]{2,1,0:T(8,128)(2,1)}), bf16[32,128,128]{2,1,0:T(8,128)(2,1)}, u32[]{:S(2)}, u32[]{:S(2)}) %all-to-all-start) | async-done | bytes 1048608 | tf_op jit(solution)/shard_map/all_to_all | solution.py:102
  77.2 4.7 %all-to-all-start.2 = ((bf16[32,128,128]{2,1,0:T(8,128)(2,1)}), bf16[32,128,128]{2,1,0:T(8,128)(2,1)}, u32[]{:S(2)}, u32[]{:S(2)}) async-start(bf16[32,128,128]{2,1,0:T(8,128)(2,1)} %copy.87), calls=%async_computation.2 | async-start | bytes 2097152 | tf_op jit(solution)/shard_map/all_to_all | solution.py:102
  81.8 86.3 %all-gather.3.cloned.1.call-done = bf16[1,2048,3072]{2,1,0:T(8,128)(2,1)} async-done(((bf16[1,64,3072]{2,1,0:T(8,128)(2,1)}), bf16[1,2048,3072]{2,1,0:T(8,128)(2,1)}) %all-gather.3.cloned.1.call-update) | async-done | bytes 12582928 | tf_op jit(solution)/shard_map/all_gather | solution.py:111
  168.1 8.5 %fusion.6 = bf16[32,8,16,128]{3,1,2,0:T(8,128)(2,1)S(1)} fusion(bf16[256,3072]{1,0:T(8,128)(2,1)} %bitcast.96, bf16[1,2048,3072]{2,1,0:T(8,128)(2,1)} %all-gather.3.cloned.1.call-done), kind=kOutput, calls=%fused_computation.7 | convolution fusion | flops 3221749760 | bytes 15204352 | tf_op jit(solution)/shard_map/dot_general | solution.py:18
  176.6 0.2 copy.101
  176.9 0.6 fusion.5
  177.5 0.1 copy.90
  177.6 0.7 copy.91
  178.3 0.0 all-to-all-done.2
  178.3 5.8 %all-to-all-start.4 = ((f32[32,2,128]{2,1,0:T(2,128)}), f32[32,2,128]{2,1,0:T(2,128)S(1)}, u32[]{:S(2)}, u32[]{:S(2)}) async-start(f32[32,2,128]{2,1,0:T(2,128)} %copy.91), calls=%async_computation.4 | async-start | bytes 65536 | tf_op jit(solution)/shard_map/all_to_all | solution.py:102
  184.0 1.2 copy.88
  185.3 0.0 copy-start.3
  185.3 8.5 %all-to-all-done.4 = f32[32,2,128]{2,1,0:T(2,128)S(1)} async-done(((f32[32,2,128]{2,1,0:T(2,128)}), f32[32,2,128]{2,1,0:T(2,128)S(1)}, u32[]{:S(2)}, u32[]{:S(2)}) %all-to-all-start.4) | async-done | bytes 32800 | tf_op jit(solution)/shard_map/all_to_all | solution.py:102
  193.8 0.0 copy-start.7
  193.8 4.7 %all-to-all-start.3 = ((bf16[32,128,128]{2,1,0:T(8,128)(2,1)}), bf16[32,128,128]{2,1,0:T(8,128)(2,1)}, u32[]{:S(2)}, u32[]{:S(2)}) async-start(bf16[32,128,128]{2,1,0:T(8,128)(2,1)} %bitcast.16), calls=%async_computation.3 | async-start | bytes 2097152 | tf_op jit(solution)/shard_map/all_to_all | solution.py:102
  198.5 0.0 copy-done.3
  198.5 0.9 copy.95
  199.4 0.0 copy-done.7
  199.4 1.6 copy.96
  201.0 15.3 %all-to-all-done.3 = bf16[32,128,128]{2,1,0:T(8,128)(2,1)} async-done(((bf16[32,128,128]{2,1,0:T(8,128)(2,1)}), bf16[32,128,128]{2,1,0:T(8,128)(2,1)}, u32[]{:S(2)}, u32[]{:S(2)}) %all-to-all-start.3) | async-done | bytes 1048608 | tf_op jit(solution)/shard_map/all_to_all | solution.py:102
  216.3 3.7 %all-to-all-start.8 = ((bf16[4,2,128,768]{3,2,1,0:T(8,128)(2,1)}), bf16[4,2,128,768]{3,2,1,0:T(8,128)(2,1)S(1)}, u32[]{:S(2)}, u32[]{:S(2)}) async-start(bf16[4,2,128,768]{3,2,1,0:T(8,128)(2,1)} %bitcast.34), calls=%async_computation.8 | async-start | bytes 3145728 | tf_op jit(solution)/shard_map/all_to_all | solution.py:129
  220.0 47.2 %attention_grads.1 = (bf16[4096,128]{1,0:T(8,128)(2,1)}, bf16[4096,128]{1,0:T(8,128)(2,1)}, bf16[4096,128]{1,0:T(8,128)(2,1)}) custom-call(bf16[4096,128]{1,0:T(8,128)(2,1)} %bitcast.4.q, bf16[4096,128]{1,0:T(8,128)(2,1)} %bitcast.97, bf16[4096,128]{1,0:T(8,128)(2,1)} %bitcast.12.v, bf16[4096,128]{1,0:T(8,128)(2,1)} %bitcast.17.g, f32[2,4096]{1,0:T(2,128)} %bitcast.103), custom_call_target="tpu_custom_call" | custom-call | flops 21474836480 | bytes 8388608 | tf_op jit(solution)/shard_map/attention_grads/pallas_call | solution.py:56
  267.2 0.0 copy-start.5
  267.2 0.0 all-to-all-done.8
  267.2 24.8 %all_to_all.45 = bf16[32,128,128]{2,1,0:T(8,128)(2,1)} all-to-all(bf16[32,128,128]{2,1,0:T(8,128)(2,1)} %bitcast.100), channel_id=1, replica_groups=mesh['section'=4,'seq'=32] {'seq'}, dimensions={0} | all-to-all | bytes 2097152 | tf_op jit(solution)/shard_map/all_to_all | solution.py:102
  292.1 0.0 copy-done.5
  292.1 0.0 copy-start.9
  292.1 22.8 %all_to_all.46 = bf16[32,128,128]{2,1,0:T(8,128)(2,1)} all-to-all(bf16[32,128,128]{2,1,0:T(8,128)(2,1)S(1)} %bitcast.99), channel_id=1, replica_groups=mesh['section'=4,'seq'=32] {'seq'}, dimensions={0} | all-to-all | bytes 2097152 | tf_op jit(solution)/shard_map/all_to_all | solution.py:102
  314.8 3.9 %all-to-all-start.7 = ((bf16[32,128,128]{2,1,0:T(8,128)(2,1)}), bf16[32,128,128]{2,1,0:T(8,128)(2,1)S(1)}, u32[]{:S(2)}, u32[]{:S(2)}) async-start(bf16[32,128,128]{2,1,0:T(8,128)(2,1)} %bitcast.98), calls=%async_computation.7 | async-start | bytes 2097152 | tf_op jit(solution)/shard_map/all_to_all | solution.py:102
  318.8 0.0 copy-done.9
  318.8 0.0 copy-start.8
  318.8 2.1 gather_fusion
  320.9 0.0 copy-done.8
  320.9 3.4 multiply_convert_fusion
  324.3 0.0 copy-done.2
  324.3 1.6 copy.107
  326.0 2.3 broadcast_in_dim_reshape.10
  328.3 0.0 copy-done.1
  328.3 1.6 copy.108
  329.9 2.3 broadcast_in_dim_reshape.9
  332.2 4.5 %all-to-all-done.7 = bf16[32,128,128]{2,1,0:T(8,128)(2,1)S(1)} async-done(((bf16[32,128,128]{2,1,0:T(8,128)(2,1)}), bf16[32,128,128]{2,1,0:T(8,128)(2,1)S(1)}, u32[]{:S(2)}, u32[]{:S(2)}) %all-to-all-start.7) | async-done | bytes 1048608 | tf_op jit(solution)/shard_map/all_to_all | solution.py:102
  336.7 0.7 copy.106
  337.4 1.3 broadcast_in_dim_reshape.11
  (6 shorter events, 0.1 us)
Async XLA Ops:
  7.2 42.8 %copy-start = (f32[1,2,2,128,16]{3,4,2,1,0:T(8,128)S(1)}, f32[1,2,2,128,16]{3,4,2,1,0:T(8,128)}, u32[]{:S(2)}) copy-start(f32[1,2,2,128,16]{3,4,2,1,0:T(8,128)} %param.14) | copy-start | bytes 98308
  7.2 160.9 %all-gather.3.cloned.1.call-start = ((), (), s32[]{:S(2)}) async-start(), calls=%async_computation.9 | async-start | bytes 12976128 | tf_op jit(solution)/shard_map/all_gather | solution.py:111
  12.2 33.0 %all-to-all-start.1 = ((bf16[32,128,128]{2,1,0:T(8,128)(2,1)}), bf16[32,128,128]{2,1,0:T(8,128)(2,1)S(1)}, u32[]{:S(2)}, u32[]{:S(2)}) async-start(bf16[32,128,128]{2,1,0:T(8,128)(2,1)} %copy.85), calls=%async_computation.1 | async-start | bytes 2097152 | tf_op jit(solution)/shard_map/all_to_all | solution.py:102
  25.1 25.0 %copy-start.6 = (bf16[1,2,2,128,2048]{4,3,2,1,0:T(8,128)(2,1)S(1)}, bf16[1,2,2,128,2048]{4,3,2,1,0:T(8,128)(2,1)}, u32[]{:S(2)}) copy-start(bf16[1,2,2,128,2048]{4,3,2,1,0:T(8,128)(2,1)} %param.13) | copy-start | bytes 6291460
  45.3 7.3 %copy-start.4 = (bf16[32,128,128]{2,1,0:T(8,128)(2,1)}, bf16[32,128,128]{2,1,0:T(8,128)(2,1)S(1)}, u32[]{:S(2)}) copy-start(bf16[32,128,128]{2,1,0:T(8,128)(2,1)S(1)} %all-to-all-done.1) | copy-start | bytes 3145732
  45.3 31.9 %all-to-all-start = ((bf16[32,128,128]{2,1,0:T(8,128)(2,1)}), bf16[32,128,128]{2,1,0:T(8,128)(2,1)}, u32[]{:S(2)}, u32[]{:S(2)}) async-start(bf16[32,128,128]{2,1,0:T(8,128)(2,1)} %copy.83), calls=%async_computation | async-start | bytes 2097152 | tf_op jit(solution)/shard_map/all_to_all | solution.py:102
  77.2 101.1 %all-to-all-start.2 = ((bf16[32,128,128]{2,1,0:T(8,128)(2,1)}), bf16[32,128,128]{2,1,0:T(8,128)(2,1)}, u32[]{:S(2)}, u32[]{:S(2)}) async-start(bf16[32,128,128]{2,1,0:T(8,128)(2,1)} %copy.87), calls=%async_computation.2 | async-start | bytes 2097152 | tf_op jit(solution)/shard_map/all_to_all | solution.py:102
  178.3 15.5 %all-to-all-start.4 = ((f32[32,2,128]{2,1,0:T(2,128)}), f32[32,2,128]{2,1,0:T(2,128)S(1)}, u32[]{:S(2)}, u32[]{:S(2)}) async-start(f32[32,2,128]{2,1,0:T(2,128)} %copy.91), calls=%async_computation.4 | async-start | bytes 65536 | tf_op jit(solution)/shard_map/all_to_all | solution.py:102
  185.3 13.2 %copy-start.3 = (bf16[1,2,128,3072]{3,2,1,0:T(8,128)(2,1)S(1)}, bf16[1,2,128,3072]{3,2,1,0:T(8,128)(2,1)}, u32[]{:S(2)}) copy-start(bf16[1,2,128,3072]{3,2,1,0:T(8,128)(2,1)} %param.15) | copy-start | bytes 4718596
  193.8 5.6 %copy-start.7 = (f32[32,2,128]{2,1,0:T(2,128)}, f32[32,2,128]{2,1,0:T(2,128)S(1)}, u32[]{:S(2)}) copy-start(f32[32,2,128]{2,1,0:T(2,128)S(1)} %all-to-all-done.4) | copy-start | bytes 98308
  193.8 22.5 %all-to-all-start.3 = ((bf16[32,128,128]{2,1,0:T(8,128)(2,1)}), bf16[32,128,128]{2,1,0:T(8,128)(2,1)}, u32[]{:S(2)}, u32[]{:S(2)}) async-start(bf16[32,128,128]{2,1,0:T(8,128)(2,1)} %bitcast.16), calls=%async_computation.3 | async-start | bytes 2097152 | tf_op jit(solution)/shard_map/all_to_all | solution.py:102
  216.3 50.9 %all-to-all-start.8 = ((bf16[4,2,128,768]{3,2,1,0:T(8,128)(2,1)}), bf16[4,2,128,768]{3,2,1,0:T(8,128)(2,1)S(1)}, u32[]{:S(2)}, u32[]{:S(2)}) async-start(bf16[4,2,128,768]{3,2,1,0:T(8,128)(2,1)} %bitcast.34), calls=%async_computation.8 | async-start | bytes 3145728 | tf_op jit(solution)/shard_map/all_to_all | solution.py:129
  267.2 24.9 %copy-start.5 = (bf16[4096,128]{1,0:T(8,128)(2,1)S(1)}, bf16[4096,128]{1,0:T(8,128)(2,1)}, u32[]{:S(2)}) copy-start(bf16[4096,128]{1,0:T(8,128)(2,1)} %get-tuple-element.7) | copy-start | bytes 3145732
  292.1 26.7 %copy-start.9 = (s32[5]{0:T(128)S(1)}, s32[5]{0:T(128)}, u32[]{:S(2)}) copy-start(s32[5]{0:T(128)} %param.18) | copy-start | bytes 64
  314.8 21.9 %all-to-all-start.7 = ((bf16[32,128,128]{2,1,0:T(8,128)(2,1)}), bf16[32,128,128]{2,1,0:T(8,128)(2,1)S(1)}, u32[]{:S(2)}, u32[]{:S(2)}) async-start(bf16[32,128,128]{2,1,0:T(8,128)(2,1)} %bitcast.98), calls=%async_computation.7 | async-start | bytes 2097152 | tf_op jit(solution)/shard_map/all_to_all | solution.py:102
  318.8 2.1 copy-start.8
  320.9 3.4 copy-start.2
  324.3 3.9 %copy-start.1 = (bf16[32,128,128]{2,1,0:T(8,128)(2,1)S(1)}, bf16[32,128,128]{2,1,0:T(8,128)(2,1)}, u32[]{:S(2)}) copy-start(bf16[32,128,128]{2,1,0:T(8,128)(2,1)} %all_to_all.46) | copy-start | bytes 3145732
Sparse Core Ops, SparseCore 0:
  11.0 157.0 all-gather.2

commit v2 on v1

v2 whole, which is shorter than its diff:
```python
import functools
import math

import jax
import jax.numpy as jnp
from jax import lax
from jax.experimental import pallas as pl
from jax.experimental.pallas import tpu as pltpu
from jax.sharding import PartitionSpec as P

F32 = jnp.float32
BF16 = jnp.bfloat16
NT = (((1,), (1,)), ((), ()))
NN = (((1,), (0,)), ((), ()))


def dot(a, b, dims):
    return lax.dot_general(a, b, dims, preferred_element_type=F32)


def ring_offset(i):
    return i + (i // 2) * (1 - 2 * (i % 2))


def kernel(
    plan,
    control_map,
    control_scale,
    q_in,
    k_in,
    v_in,
    o_in,
    lse_in,
    cot_in,
    w_in,
    dq_out,
    dk_out,
    dv_out,
    control_out,
    q_two,
    k_two,
    v_two,
    o_two,
    lse_two,
    cot,
    w,
    q_send,
    k_send,
    v_send,
    g_send,
    stat_send,
    q,
    k,
    v,
    g,
    stat,
    lse_row,
    delta_row,
    dq_sum,
    pieces,
    load_sem,
    swap_s,
    swap_r,
    ring_s,
    ring_r,
    heads_s,
    heads_r,
    back_s,
    back_r,
    own_sem,
    piece_s,
    piece_r,
):
    me = lax.axis_index("seq")
    section = lax.axis_index("section")
    z, y, x = me // 8, (me // 2) % 4, me % 2
    devices, rows, head_size = q.shape
    heads = devices // 2
    half_rows = rows // 2
    half_depth = w.shape[4]
    scale = head_size**-0.5
    scale2 = scale * math.log2(math.e)

    def index_of(z, y, x):
        return ((z + 4) % 4) * 8 + ((y + 4) % 4) * 2 + x % 2

    def peer(step):
        return index_of(z + step // 8, y + (step // 2) % 4, x + step % 2)

    def columns(head):
        return pl.ds(pl.multiple_of(head * head_size, head_size), head_size)

    def remote(src, dst, send, recv, device):
        return pltpu.make_async_remote_copy(
            src_ref=src,
            dst_ref=dst,
            send_sem=send,
            recv_sem=recv,
            device_id=device,
            device_id_type=pl.DeviceIdType.MESH,
        )

    def local(src, dst, sem):
        return pltpu.make_async_copy(src, dst, sem)

    loads = [
        local(src, dst, load_sem.at[i])
        for i, (src, dst) in enumerate(
            ((k_in, k_two), (q_in, q_two), (v_in, v_two), (o_in, o_two), (lse_in, lse_two), (cot_in, cot))
        )
    ]
    for load in loads:
        load.start()
    my_rows = pl.ds(pl.multiple_of(x * half_rows, half_rows), half_rows)
    other_rows = pl.ds(pl.multiple_of((1 - x) * half_rows, half_rows), half_rows)

    def part_columns(part):
        return pl.ds(part * half_depth, half_depth)

    own_w = [local(w_in.at[:, part_columns(p)], w.at[p, z, y, my_rows], load_sem.at[6 + p]) for p in range(2)]
    for copy in own_w:
        copy.start()
    barrier = pltpu.get_barrier_semaphore()

    @pl.loop(1, devices)
    def _(step):
        pl.semaphore_signal(
            barrier, inc=1, device_id={"seq": peer(step)}, device_id_type=pl.DeviceIdType.MESH
        )

    @pl.loop(1, 4)
    def _(step):
        pl.semaphore_signal(
            barrier, inc=1, device_id={"section": (section + step) % 4}, device_id_type=pl.DeviceIdType.MESH
        )

    pl.semaphore_wait(barrier, devices + 2)

    swaps = [
        remote(
            w_in.at[:, part_columns(p)], w.at[p, z, y, my_rows], swap_s.at[p], swap_r.at[p], {"seq": index_of(z, y, x + 1)}
        )
        for p in range(2)
    ]
    for copy in swaps:
        copy.start()

    def turn(part, first, second):
        return (first, second) if part == 0 else (second, first)

    def block(part, first, second):
        dz, dy = turn(part, first, second)
        return w.at[part, (z + dz + 4) % 4, (y + dy + 4) % 4]

    def hop(part, where, to, rows_of, sem, src=None):
        dst = block(part, *where)
        if rows_of is not None:
            dst = dst.at[rows_of]
        dz, dy = turn(part, *to)
        return remote(
            dst if src is None else src,
            dst,
            ring_s.at[part, sem],
            ring_r.at[part, sem],
            {"seq": index_of(z + dz, y + dy, x)},
        )

    low, high = pl.ds(0, half_rows), pl.ds(half_rows, half_rows)
    first, second, forward = {}, {}, {}
    for p in range(2):
        src = w_in.at[:, part_columns(p)]
        first[p] = [hop(p, (0, 0), (1, 0), my_rows, 0, src), hop(p, (0, 0), (-1, 0), my_rows, 1, src)]
        for copy in first[p]:
            copy.start()

    def select(two, send, held, sem):
        picked = plan[0]

        @pl.loop(0, 2)
        def _(image):
            for head in range(heads):
                send[image * heads + head] = two[picked, image, :, head * head_size : (head + 1) * head_size]

        held[me] = send[me]

        @pl.loop(1, devices)
        def _(step):
            to = peer(step)
            remote(send.at[to], held.at[me], heads_s.at[sem], heads_r.at[sem], {"seq": to}).start()

    def arrived(send, held, sem):
        some = pl.ds(0, devices - 1)
        local(held.at[some], held.at[some], heads_r.at[sem]).wait()
        local(send.at[some], send.at[some], heads_s.at[sem]).wait()

    loads[0].wait()
    select(k_two, k_send, k, 0)
    loads[1].wait()
    select(q_two, q_send, q, 1)

    def start_second(p, group):
        at = ring_offset(group)
        second[p, group] = [
            hop(p, (at, 0), (0, 1), None, 6 + 4 * group),
            hop(p, (at, 0), (0, -1), None, 7 + 4 * group),
        ]
        for copy in second[p, group]:
            copy.start()

    for copy in own_w:
        copy.wait()
    for p in range(2):
        swaps[p].wait_recv()
        first[p] += [hop(p, (0, 0), (1, 0), other_rows, 2), hop(p, (0, 0), (-1, 0), other_rows, 3)]
        for copy in first[p][2:]:
            copy.start()
        start_second(p, 0)
    loads[2].wait()
    select(v_two, v_send, v, 2)
    for load in loads[3:]:
        load.wait()
    for p in range(2):
        first[p][0].wait_recv()
        first[p][2].wait_recv()
        first[p].append(hop(p, (-1, 0), (1, 0), low, 4))
        first[p][4].start()
        first[p][1].wait_recv()
        first[p][3].wait_recv()
        first[p].append(hop(p, (1, 0), (-1, 0), high, 5))
        first[p][5].start()
    for p in range(2):
        start_second(p, 1)
        start_second(p, 2)

    def start_forward(group):
        at = ring_offset(group)
        for p in range(2):
            second[p, group][0].wait_recv()
            forward[p, group] = [hop(p, (at, -1), (0, 1), low, 8 + 4 * group)]
            forward[p, group][0].start()
            second[p, group][1].wait_recv()
            forward[p, group].append(hop(p, (at, 1), (0, -1), high, 9 + 4 * group))
            forward[p, group][1].start()

    def project(dz, dy):
        zz, yy = (z + dz + 4) % 4, (y + dy + 4) % 4
        head = zz * 4 + yy
        c = cot[...].reshape(2 * rows, 2 * half_depth)
        grad = dot(c[:, :half_depth], w[0, zz, yy], NT) + dot(c[:, half_depth:], w[1, zz, yy], NT)
        grad = grad.astype(BF16)
        picked = plan[0]
        for image in range(2):
            to = image * heads + head
            grad_rows = grad[image * rows : (image + 1) * rows]
            g_send[to] = grad_rows
            products = grad_rows.astype(F32) * o_two[picked, image, :, columns(head)].astype(F32)
            delta = jnp.sum(products.T, axis=0, keepdims=True)
            lse = lse_two[picked, image, pl.ds(head, 1), :] * math.log2(math.e)
            row = lax.broadcasted_iota(jnp.int32, (8, rows), 0)
            stat_send[to] = jnp.where(row == 0, lse, delta)

            @pl.when(to != me)
            def _():
                remote(g_send.at[to], g.at[me], heads_s.at[3], heads_r.at[3], {"seq": to}).start()
                remote(stat_send.at[to], stat.at[me], heads_s.at[4], heads_r.at[4], {"seq": to}).start()

            @pl.when(to == me)
            def _():
                g[me] = g_send[me]
                stat[me] = stat_send[me]

    def project_group(group):
        at = ring_offset(group)

        @pl.loop(0, group + 1)
        def _(n):
            project(at, ring_offset(n))

        if group > 0:

            @pl.loop(0, group)
            def _(n):
                project(ring_offset(n), at)

    project_group(0)
    start_forward(0)
    for p in range(2):
        first[p][4].wait_recv()
        first[p][5].wait_recv()
        start_second(p, 3)
    for group in range(1, 4):
        start_forward(group)
        if group > 1:
            project_group(group - 1)
        for p in range(2):
            for copy in forward[p, group - 1]:
                copy.wait_recv()
    for p in range(2):
        for copy in forward[p, 3]:
            copy.wait_recv()
    project_group(3)

    channels = pieces.shape[3]

    def piece(to):
        return cot.at[:, :, pl.ds(pl.multiple_of(to * channels, channels), channels)]

    own_piece = local(piece(section), pieces.at[section], own_sem.at[3])
    own_piece.start()

    @pl.loop(1, 4)
    def _(step):
        to = (section + step) % 4
        remote(piece(to), pieces.at[section], piece_s, piece_r, {"section": to}).start()

    for sem, (send, held) in enumerate(((k_send, k), (q_send, q), (v_send, v), (g_send, g), (stat_send, stat))):
        arrived(send, held, sem)

    for source in range(devices):
        lse_row[:, source * rows : (source + 1) * rows] = stat[source, 0:1, :]
        delta_row[:, source * rows : (source + 1) * rows] = stat[source, 1:2, :]

    total = devices * rows
    my_image, my_columns = me // heads, columns(me % heads)

    def give_back(send, out, sem, source):
        place = out.at[my_image, :, my_columns]

        @pl.when(source != me)
        def _():
            remote(send.at[source], place, back_s.at[sem], back_r.at[sem], {"seq": source}).start()

        @pl.when(source == me)
        def _():
            local(send.at[source], place, own_sem.at[sem]).start()

    dq_sum[...] = jnp.zeros_like(dq_sum)
    key_blocks = 8
    query_blocks = 4

    @pl.loop(0, devices // key_blocks)
    def _(u):
        us = pl.ds(u * key_blocks, key_blocks)
        kb = k[us].reshape(key_blocks * rows, head_size)
        vb = v[us].reshape(key_blocks * rows, head_size)
        kt = kb.T

        def inner(t, carry):
            sum_k, sum_v = carry
            qb = q[pl.ds(t * query_blocks, query_blocks)].reshape(query_blocks * rows, head_size)
            gb = g[pl.ds(t * query_blocks, query_blocks)].reshape(query_blocks * rows, head_size)
            ts = pl.ds(pl.multiple_of(t * query_blocks * rows, query_blocks * rows), query_blocks * rows)
            p = jnp.exp2(dot(kb, qb, NT) * scale2 - lse_row[:, ts])
            sum_v = sum_v + dot(p.astype(BF16), gb, NN)
            ds = (p * (dot(vb, gb, NT) - delta_row[:, ts])).astype(BF16)
            sum_k = sum_k + dot(ds, qb, NN)
            dq_sum[:, ts] += dot(kt, ds, NN)
            return sum_k, sum_v

        zeros = jnp.zeros((key_blocks * rows, head_size), F32)
        sum_k, sum_v = lax.fori_loop(0, devices // query_blocks, inner, (zeros, zeros), unroll=4)
        k_send[us] = (sum_k * scale).astype(BF16).reshape(key_blocks, rows, head_size)
        v_send[us] = sum_v.astype(BF16).reshape(key_blocks, rows, head_size)

        @pl.loop(0, key_blocks)
        def _(n):
            give_back(k_send, dk_out, 0, u * key_blocks + n)
            give_back(v_send, dv_out, 1, u * key_blocks + n)

    for source in range(devices):
        q_send[source] = (dq_sum[:, source * rows : (source + 1) * rows] * scale).T.astype(BF16)
        give_back(q_send, dq_out, 2, source)

    own_piece.wait()
    three = pl.ds(0, 3)
    local(pieces.at[three], pieces.at[three], piece_r).wait()
    local(pieces.at[three], pieces.at[three], piece_s).wait()
    for j in range(control_out.shape[0]):
        source, factor = control_map[j], control_scale[j]
        for image in range(2):
            control_out[j, image] = (factor * pieces[source, image].astype(F32)).astype(BF16)

    for copies in list(first.values()) + list(second.values()) + list(forward.values()) + [swaps]:
        for copy in copies:
            copy.wait_send()
    some = pl.ds(0, devices - 1)
    for sem, (send, out) in enumerate(((k_send, dk_out), (v_send, dv_out), (q_send, dq_out))):
        local(send.at[some], send.at[some], back_s.at[sem]).wait()
        local(send.at[some], send.at[some], back_r.at[sem]).wait()
        local(send.at[me], out.at[my_image, :, my_columns], own_sem.at[sem]).wait()


def shards(
    saved_q,
    saved_k,
    saved_v,
    saved_o,
    saved_lse,
    cotangent,
    out_weight,
    plan,
    control_map,
    control_scale,
):
    micro, images, rows, width = saved_q.shape[1:]
    head_count = saved_lse.shape[4]
    head_size = width // head_count
    devices = images * head_count
    depth = cotangent.shape[3]
    sections = lax.axis_size("section")
    channels = depth // sections
    controls = control_map.shape[0]
    rows_out = jax.ShapeDtypeStruct((images, rows, width), BF16)
    two = pltpu.VMEM((micro, images, rows, width), BF16)
    blocks = pltpu.VMEM((devices, rows, head_size), BF16)
    stats = pltpu.VMEM((devices, 8, rows), F32)
    row = pltpu.VMEM((1, devices * rows), F32)
    anywhere = pl.BlockSpec(memory_space=pl.ANY)
    scalars = pl.BlockSpec(memory_space=pltpu.SMEM)
    dma = pltpu.SemaphoreType.DMA
    total = devices * rows
    dq, dk, dv, control = pl.pallas_call(
        kernel,
        out_shape=(
            rows_out,
            rows_out,
            rows_out,
            jax.ShapeDtypeStruct((controls, images, rows, channels), BF16),
        ),
        in_specs=[scalars] * 3 + [anywhere] * 7,
        out_specs=(anywhere, anywhere, anywhere, pl.BlockSpec(memory_space=pltpu.VMEM)),
        scratch_shapes=[two] * 4
        + [
            pltpu.VMEM((micro, images, head_count, rows), F32),
            pltpu.VMEM((images, rows, depth), BF16),
            pltpu.VMEM((2, 4, 4, rows, depth // 2), BF16),
        ]
        + [blocks] * 4
        + [stats]
        + [blocks] * 4
        + [stats, row, row]
        + [
            pltpu.VMEM((head_size, total), F32),
            pltpu.VMEM((sections, images, rows, channels), BF16),
            dma((8,)),
            dma((2,)),
            dma((2,)),
            dma((2, 22)),
            dma((2, 22)),
            dma((5,)),
            dma((5,)),
            dma((3,)),
            dma((3,)),
            dma((4,)),
            dma(()),
            dma(()),
        ],
        compiler_params=pltpu.CompilerParams(
            collective_id=0, has_side_effects=True, vmem_limit_bytes=58 * 2**20
        ),
        cost_estimate=pl.CostEstimate(
            flops=10 * total * total * head_size, bytes_accessed=32 * total * head_size, transcendentals=0
        ),
        name="attention_backward",
    )(
        plan,
        control_map,
        control_scale,
        saved_q[0],
        saved_k[0],
        saved_v[0],
        saved_o[0],
        saved_lse[0].transpose(0, 1, 3, 2),
        cotangent[0],
        out_weight[0],
    )
    return (dq[None], dk[None], dv[None], control)


def solution(mesh):
    placed = (
        P("section", None, None, "seq", None),
        P("section", None, None, "seq", None),
        P("section", None, None, "seq", None),
        P("section", None, None, "seq", None),
        P("section", None, None, "seq", None),
        P("section", None, "seq", None),
        P("section", "seq", None),
        P("section"),
        P(),
        P(),
    )
    return jax.shard_map(
        shards,
        mesh=mesh,
        in_specs=placed,
        out_specs=(
            P("section", None, "seq", None),
            P("section", None, "seq", None),
            P("section", None, "seq", None),
            P(None, None, "seq", "section"),
        ),
        check_vma=False,
    )
```

time: 347 us -> 214 us (0.62)
  Pallas kernels: 47.2 us -> 206 us
  waiting for transfers between devices: 157 us -> 0 us
  blocking collectives: 47.6 us -> 0 us
  starting transfers between devices: 38.3 us -> 0 us
  local copies, waits for them, and re-layouts: 25.8 us -> 5.67 us
  between operations: 14.9 us -> 1.31 us
  matrix products: 8.5 us -> 0 us
  other arithmetic: 6.61 us -> 0 us
    pallas_call x1, Pallas kernels: 47.2 us -> 206 us  [shards(): pl.pallas_call(kernel, out_shape=(rows_out, rows_out, rows_out, jax.Shape...]
    all_gather x1 -> x0, waiting for transfers between devices: 86.3 us -> none  [shards(): weight = lax.all_gather(out_weight[0], 'seq', axis=0, tiled=True)]
    all_to_all x7 -> x0, waiting for transfers between devices: 69.6 us -> none  [the longest x6 69.6 us: exchange(): return lax.all_to_all(array, 'seq', split_axis=0, concat_axis=0, tiled=True)]
    all_to_all x2 -> x0, blocking collectives: 47.6 us -> none  [exchange(): return lax.all_to_all(array, 'seq', split_axis=0, concat_axis=0, tiled=True)]
    all_to_all x7 -> x0, starting transfers between devices: 38.3 us -> none  [the longest x6 34.6 us: exchange(): return lax.all_to_all(array, 'seq', split_axis=0, concat_axis=0, tiled=True)]
    another operation x5 -> x0, local copies, waits for them, and re-layouts: 8.67 us -> none  [the longest x3 5.86 us: shards(): to_tokens(exchange(grad.reshape(-1, local_rows, head_size)), images)[None]]
    reshape x7 -> x0, local copies, waits for them, and re-layouts: 8.57 us -> none  [the longest x3 3.98 us: to_tokens(): array.reshape(images, head_count, rows, head_size).transpose(0, 2, 1, 3)]
    dot_general x1 -> x0, matrix products: 8.5 us -> none  [dot(): return lax.dot_general(a, b, dims, preferred_element_type=F32)]
  transfers between devices with their start and end apart: 8 -> 0, of which waited for: 6 -> 0; matrix products, arithmetic and copies ran while one was open for 11% -> 0% of each run, Pallas kernels for 14% -> 0%
where the time goes in v2:
time: 214 us; the launch traced here: 213 us
  Pallas kernels  206 us (96%)
  local copies, waits for them, and re-layouts  5.67 us (3%)
    pallas_call x1, Pallas kernels, shards(): pl.pallas_call(kernel, out_shape=(rows_out, rows_out, rows_out, jax.Shape...  206 us
    unnamed x10, local copies, waits for them, and re-layouts  5.67 us

profile of v2, /device:TPU:0, one launch (start us, length us, event | category | flops | bytes accessed | tf_op | source)
XLA Modules:
  0.0 213.2 jit_solution(7974117554247218576)
XLA Ops:
  1.3 206.2 %attention_backward.1 = (bf16[2,128,2048]{2,1,0:T(8,128)(2,1)}, bf16[2,128,2048]{2,1,0:T(8,128)(2,1)}, bf16[2,128,2048]{2,1,0:T(8,128)(2,1)}, bf16[5,2,128,768]{3,2,1,0:T(8,128)(2,1)}) custom-call(s32[1]{0:T(128)S(6)} %copy.18.plan, s32[5]{0:T(128)} %control_map.1, f32[5]{0:T(128)} %control_scale.1, bf16[2,2,128,2048]{3,2,1,0:T(8,128)(2,1)} %bitcast.15, ...), custom_call_target="tpu_custom_call" | custom-call | flops 21474836480 | bytes 16777216 | tf_op jit(solution)/shard_map/attention_backward/pallas_call | solution.py:422
  207.5 0.0 copy-start.2
  207.5 0.0 copy-start.1
  207.5 2.5 %copy.19 = bf16[1,2,128,2048]{3,2,1,0:T(8,128)(2,1)} copy(bf16[1,2,128,2048]{3,2,1,0:T(8,128)(2,1)} %bitcast.14) | data formatting | bytes 2097152
  210.0 0.0 copy-done.2
  210.0 0.0 copy-start
  210.0 1.0 copy.20
  211.0 0.0 copy-done.1
  211.0 1.0 copy.21
  211.9 0.0 copy-done
  211.9 1.3 copy.22
Async XLA Ops:
  207.5 2.5 %copy-start.2 = (bf16[2,128,2048]{2,1,0:T(8,128)(2,1)S(1)}, bf16[2,128,2048]{2,1,0:T(8,128)(2,1)}, u32[]{:S(2)}) copy-start(bf16[2,128,2048]{2,1,0:T(8,128)(2,1)} %get-tuple-element.9) | copy-start | bytes 3145732
  207.5 3.4 %copy-start.1 = (bf16[2,128,2048]{2,1,0:T(8,128)(2,1)S(1)}, bf16[2,128,2048]{2,1,0:T(8,128)(2,1)}, u32[]{:S(2)}) copy-start(bf16[2,128,2048]{2,1,0:T(8,128)(2,1)} %get-tuple-element.10) | copy-start | bytes 3145732
  210.0 1.9 copy-start

commit v3 on v2

v3 whole, which is shorter than its diff:
```python
import functools
import math

import jax
import jax.numpy as jnp
from jax import lax
from jax.experimental import pallas as pl
from jax.experimental.pallas import tpu as pltpu
from jax.sharding import PartitionSpec as P

F32 = jnp.float32
BF16 = jnp.bfloat16
NT = (((1,), (1,)), ((), ()))
NN = (((1,), (0,)), ((), ()))


def dot(a, b, dims):
    return lax.dot_general(a, b, dims, preferred_element_type=F32)


def ring_offset(i):
    return i + (i // 2) * (1 - 2 * (i % 2))


def kernel(
    plan,
    control_map,
    control_scale,
    q_in,
    k_in,
    v_in,
    o_in,
    lse_in,
    cot_in,
    w_in,
    dq_out,
    dk_out,
    dv_out,
    control_out,
    first_two,
    second_two,
    lse_two,
    cot,
    w,
    q_send,
    k_send,
    v_send,
    o_send,
    stat_send,
    q,
    k,
    v,
    o,
    g,
    stat,
    lse_row,
    delta_row,
    kept,
    dq_sum,
    pieces,
    load_sem,
    swap_s,
    swap_r,
    ring_s,
    ring_r,
    heads_s,
    heads_r,
    back_s,
    back_r,
    own_sem,
    piece_s,
    piece_r,
):
    me = lax.axis_index("seq")
    section = lax.axis_index("section")
    z, y, x = me // 8, (me // 2) % 4, me % 2
    devices, rows, head_size = q.shape
    heads = devices // 2
    half_rows, half_depth = w.shape[3:]
    scale = head_size**-0.5
    scale2 = scale * math.log2(math.e)

    def index_of(z, y, x):
        return ((z + 4) % 4) * 8 + ((y + 4) % 4) * 2 + x % 2

    def peer(slot):
        run, dz = slot // 4, slot % 4
        return index_of(z + dz, y + dz + run // 2, x + run + dz)

    def slot_at(to):
        dz, dy, dx = z - to // 8 + 4, y - (to // 2) % 4 + 4, x - to % 2 + 2
        return (((dy - dz + 8) % 4) * 2 + (dx + dz) % 2) * 4 + dz % 4

    def columns(head):
        return pl.ds(pl.multiple_of(head * head_size, head_size), head_size)

    def remote(src, dst, send, recv, device):
        return pltpu.make_async_remote_copy(
            src_ref=src,
            dst_ref=dst,
            send_sem=send,
            recv_sem=recv,
            device_id=device,
            device_id_type=pl.DeviceIdType.MESH,
        )

    def local(src, dst, sem):
        return pltpu.make_async_copy(src, dst, sem)

    loads = [
        local(src, dst, load_sem.at[i])
        for i, (src, dst) in enumerate(
            (
                (k_in, first_two),
                (q_in, second_two),
                (lse_in, lse_two),
                (v_in, first_two),
                (o_in, second_two),
                (cot_in, cot.at[0]),
            )
        )
    ]
    for i in (0, 1, 2, 5):
        loads[i].start()

    def part_columns(part):
        return pl.ds(part * half_depth, half_depth)

    own_w = [local(w_in.at[:, part_columns(p)], w.at[p, z, y], load_sem.at[6 + p]) for p in range(2)]
    for copy in own_w:
        copy.start()
    barrier = pltpu.get_barrier_semaphore()

    @pl.loop(1, devices)
    def _(step):
        pl.semaphore_signal(
            barrier, inc=1, device_id={"seq": peer(step)}, device_id_type=pl.DeviceIdType.MESH
        )

    @pl.loop(1, 4)
    def _(step):
        pl.semaphore_signal(
            barrier, inc=1, device_id={"section": (section + step) % 4}, device_id_type=pl.DeviceIdType.MESH
        )

    pl.semaphore_wait(barrier, devices + 2)

    def turn(part, first, second):
        return (first, second) if part == 0 else (second, first)

    def block(part, first, second):
        dz, dy = turn(part, first, second)
        return w.at[part, (z + dz + 4) % 4, (y + dy + 4) % 4]

    def hop(part, where, to, rows_of, sem, src=None):
        dst = block(part, *where)
        if rows_of is not None:
            dst = dst.at[rows_of]
        dz, dy = turn(part, *to)
        return remote(
            dst if src is None else src,
            dst,
            ring_s.at[part, sem],
            ring_r.at[part, sem],
            {"seq": index_of(z + dz, y + dy, x)},
        )

    low, high = pl.ds(0, half_rows // 2), pl.ds(half_rows // 2, half_rows // 2)
    first, second, forward = {}, {}, {}
    def start_second(p, group):
        at = ring_offset(group)
        src = w_in.at[:, part_columns(p)] if group == 0 else None
        second[p, group] = [
            hop(p, (at, 0), (0, 1), None, 4 + 4 * group, src),
            hop(p, (at, 0), (0, -1), None, 5 + 4 * group, src),
        ]
        for copy in second[p, group]:
            copy.start()

    for p in range(2):
        src = w_in.at[:, part_columns(p)]
        first[p] = [hop(p, (0, 0), (1, 0), None, 0, src), hop(p, (0, 0), (-1, 0), None, 1, src)]
        for copy in first[p]:
            copy.start()
    swap = remote(cot_in, cot.at[1], swap_s, swap_r, {"seq": index_of(z, y, x + 1)})
    swap.start()
    for p in range(2):
        start_second(p, 0)

    def select(two, send, held, sem):
        picked = plan[0]

        @pl.loop(0, 2)
        def _(image):
            for head in range(heads):
                send[image * heads + head] = two[picked, image, :, head * head_size : (head + 1) * head_size]

        held[0] = send[me]

        @pl.loop(1, devices)
        def _(step):
            to = peer(step)
            remote(send.at[to], held.at[slot_at(to)], heads_s.at[sem], heads_r.at[sem], {"seq": to}).start()

    some = pl.ds(0, devices - 1)

    def sent(send, sem):
        local(send.at[some], send.at[some], heads_s.at[sem]).wait()

    def arrived(held, sem):
        local(held.at[some], held.at[some], heads_r.at[sem]).wait()

    loads[0].wait()
    select(first_two, k_send, k, 0)
    loads[1].wait()
    select(second_two, q_send, q, 1)
    loads[2].wait()
    for image in range(2):
        for head in range(heads):
            lse = lse_two[plan[0], image, head : head + 1, :] * math.log2(math.e)
            stat_send[image * heads + head] = jnp.broadcast_to(lse, (8, rows))
    stat[0] = stat_send[me]

    @pl.loop(1, devices)
    def _(step):
        to = peer(step)
        remote(stat_send.at[to], stat.at[slot_at(to)], heads_s.at[5], heads_r.at[5], {"seq": to}).start()

    loads[3].start()
    loads[4].start()
    for copy in own_w:
        copy.wait()
    for p in range(2):
        first[p][0].wait_recv()
        first[p].append(hop(p, (-1, 0), (1, 0), low, 2))
        first[p][2].start()
        first[p][1].wait_recv()
        first[p].append(hop(p, (1, 0), (-1, 0), high, 3))
        first[p][3].start()
    for p in range(2):
        start_second(p, 1)
        start_second(p, 2)
    loads[3].wait()
    select(first_two, v_send, v, 2)

    def start_forward(group):
        at = ring_offset(group)
        for p in range(2):
            second[p, group][0].wait_recv()
            forward[p, group] = [hop(p, (at, -1), (0, 1), low, 6 + 4 * group)]
            forward[p, group][0].start()
            second[p, group][1].wait_recv()
            forward[p, group].append(hop(p, (at, 1), (0, -1), high, 7 + 4 * group))
            forward[p, group][1].start()

    start_forward(0)
    for p in range(2):
        first[p][2].wait_recv()
        first[p][3].wait_recv()
        start_second(p, 3)
    loads[4].wait()
    select(second_two, o_send, o, 3)
    for group in range(1, 4):
        start_forward(group)
    for group in range(4):
        for p in range(2):
            for copy in forward[p, group]:
                copy.wait_recv()
    loads[5].wait()
    swap.wait_recv()

    sent(k_send, 0)
    g_send = k_send

    lane = lax.broadcasted_iota(jnp.int32, (rows, head_size), 1)

    @pl.loop(0, 4)
    def _(zz):
        c = cot[...].reshape(4 * rows, 2 * half_depth)
        w0 = w[0, zz].reshape(4 * half_rows, half_depth)
        w1 = w[1, zz].reshape(4 * half_rows, half_depth)
        grad = dot(c[:, :half_depth], w0, NT) + dot(c[:, half_depth:], w1, NT)
        for image in range(2):
            for pair in range(2):
                cols = slice(pair * head_size, (pair + 1) * head_size)
                mine = grad[image * rows : (image + 1) * rows, cols]
                other = grad[(2 + image) * rows : (3 + image) * rows, cols]
                even = jnp.where(lane < head_size // 2, mine, pltpu.roll(other, head_size // 2, 1))
                odd = jnp.where(lane < head_size // 2, pltpu.roll(mine, head_size // 2, 1), other)
                for n, half in enumerate((even, odd)):
                    to = image * heads + zz * 4 + pair * 2 + n
                    g_send[to] = half.astype(BF16)

                    @pl.when(to != me)
                    def _():
                        remote(
                            g_send.at[to], g.at[slot_at(to)], heads_s.at[4], heads_r.at[4], {"seq": to}
                        ).start()

                    @pl.when(to == me)
                    def _():
                        g[0] = g_send[me]

    channels = pieces.shape[3]

    def piece(to):
        return cot.at[0, :, :, pl.ds(pl.multiple_of(to * channels, channels), channels)]

    own_piece = local(piece(section), pieces.at[section], own_sem.at[3])
    own_piece.start()

    @pl.loop(1, 4)
    def _(step):
        to = (section + step) % 4
        remote(piece(to), pieces.at[section], piece_s, piece_r, {"section": to}).start()

    key_blocks = 4
    query_blocks = 8
    key_rows = key_blocks * rows
    query_rows = query_blocks * rows

    def keys_of(ref, u):
        return ref[pl.ds(u * key_blocks, key_blocks)].reshape(key_rows, head_size)

    def queries_of(ref, t):
        return ref[pl.ds(t * query_blocks, query_blocks)].reshape(query_rows, head_size)

    def row_of(ref, t):
        return ref[:, pl.ds(pl.multiple_of(t * query_rows, query_rows), query_rows)]

    def probabilities(kb, qb, t):
        return jnp.exp2(dot(kb, qb, NT) * scale2 - row_of(lse_row, t))

    arrived(k, 0)
    arrived(q, 1)
    arrived(stat, 5)
    for source in range(devices):
        lse_row[:, source * rows : (source + 1) * rows] = stat[source, 0:1, :]

    @pl.loop(0, kept.shape[0])
    def _(u):
        kb = keys_of(k, u)

        def keep(t, carry):
            kept[u, t] = probabilities(kb, queries_of(q, t), t).astype(BF16)
            return carry

        lax.fori_loop(0, devices // query_blocks, keep, 0, unroll=4)

    arrived(v, 2)
    arrived(o, 3)
    arrived(g, 4)
    for sem, send in ((1, q_send), (2, v_send), (3, o_send), (4, g_send), (5, stat_send)):
        sent(send, sem)

    low_lane = lane < head_size // 2
    for pair in range(devices // 2):
        slots = (pair // 4 * 8 + pair % 4, pair // 4 * 8 + pair % 4 + 4)
        a, b = g[slots[0]].astype(F32), g[slots[1]].astype(F32)
        straight = ((x + pair % 4) % 2) == 0
        one, two = jnp.where(low_lane, a, b), jnp.where(low_lane, b, a)
        one = jnp.where(straight, one, pltpu.roll(one, head_size // 2, 1))
        two = jnp.where(straight, pltpu.roll(two, head_size // 2, 1), two)
        for slot, joined in zip(slots, (one, two)):
            g[slot] = joined.astype(BF16)
            products = joined * o[slot].astype(F32)
            delta_row[:, slot * rows : (slot + 1) * rows] = jnp.sum(products.T, axis=0, keepdims=True)

    total = devices * rows
    my_image, my_columns = me // heads, columns(me % heads)

    def give_back(send, out, sem, slot):
        place = out.at[my_image, :, my_columns]

        @pl.when(slot != 0)
        def _():
            remote(send.at[slot], place, back_s.at[sem], back_r.at[sem], {"seq": peer(slot)}).start()

        @pl.when(slot == 0)
        def _():
            local(send.at[slot], place, own_sem.at[sem]).start()

    dq_sum[...] = jnp.zeros_like(dq_sum)

    def key_block(u, have):
        kb, vb = keys_of(k, u), keys_of(v, u)
        kt = kb.T

        def inner(t, carry):
            sum_k, sum_v = carry
            qb, gb = queries_of(q, t), queries_of(g, t)
            if have:
                rounded = kept[u, t]
                p = rounded.astype(F32)
            else:
                p = probabilities(kb, qb, t)
                rounded = p.astype(BF16)
            sum_v = sum_v + dot(rounded, gb, NN)
            ds = (p * (dot(vb, gb, NT) - row_of(delta_row, t))).astype(BF16)
            sum_k = sum_k + dot(ds, qb, NN)
            dq_sum[:, pl.ds(pl.multiple_of(t * query_rows, query_rows), query_rows)] += dot(kt, ds, NN)
            return sum_k, sum_v

        zeros = jnp.zeros((key_rows, head_size), F32)
        sum_k, sum_v = lax.fori_loop(0, devices // query_blocks, inner, (zeros, zeros), unroll=4)
        slots = pl.ds(u * key_blocks, key_blocks)
        k_send[slots] = (sum_k * scale).astype(BF16).reshape(key_blocks, rows, head_size)
        v_send[slots] = sum_v.astype(BF16).reshape(key_blocks, rows, head_size)

        @pl.loop(0, key_blocks)
        def _(n):
            give_back(k_send, dk_out, 0, u * key_blocks + n)
            give_back(v_send, dv_out, 1, u * key_blocks + n)

    @pl.loop(0, kept.shape[0])
    def _(u):
        key_block(u, True)

    @pl.loop(kept.shape[0], devices // key_blocks)
    def _(u):
        key_block(u, False)

    for source in range(devices):
        q_send[source] = (dq_sum[:, source * rows : (source + 1) * rows] * scale).T.astype(BF16)
        give_back(q_send, dq_out, 2, source)

    own_piece.wait()
    three = pl.ds(0, 3)
    local(pieces.at[three], pieces.at[three], piece_r).wait()
    local(pieces.at[three], pieces.at[three], piece_s).wait()
    for j in range(control_out.shape[0]):
        source, factor = control_map[j], control_scale[j]
        for image in range(2):
            control_out[j, image] = (factor * pieces[source, image].astype(F32)).astype(BF16)

    for copies in list(first.values()) + list(second.values()) + list(forward.values()) + [[swap]]:
        for copy in copies:
            copy.wait_send()
    for sem, (send, out) in enumerate(((k_send, dk_out), (v_send, dv_out), (q_send, dq_out))):
        local(send.at[some], send.at[some], back_s.at[sem]).wait()
        local(send.at[some], send.at[some], back_r.at[sem]).wait()
        local(send.at[0], out.at[my_image, :, my_columns], own_sem.at[sem]).wait()


def shards(
    saved_q,
    saved_k,
    saved_v,
    saved_o,
    saved_lse,
    cotangent,
    out_weight,
    plan,
    control_map,
    control_scale,
):
    micro, images, rows, width = saved_q.shape[1:]
    head_count = saved_lse.shape[4]
    head_size = width // head_count
    devices = images * head_count
    depth = cotangent.shape[3]
    sections = lax.axis_size("section")
    channels = depth // sections
    controls = control_map.shape[0]
    rows_out = jax.ShapeDtypeStruct((images, rows, width), BF16)
    two = pltpu.VMEM((micro, images, rows, width), BF16)
    blocks = pltpu.VMEM((devices, rows, head_size), BF16)
    stats = pltpu.VMEM((devices, 8, rows), F32)
    row = pltpu.VMEM((1, devices * rows), F32)
    anywhere = pl.BlockSpec(memory_space=pl.ANY)
    scalars = pl.BlockSpec(memory_space=pltpu.SMEM)
    dma = pltpu.SemaphoreType.DMA
    total = devices * rows
    dq, dk, dv, control = pl.pallas_call(
        kernel,
        out_shape=(
            rows_out,
            rows_out,
            rows_out,
            jax.ShapeDtypeStruct((controls, images, rows, channels), BF16),
        ),
        in_specs=[scalars] * 3 + [anywhere] * 7,
        out_specs=(anywhere, anywhere, anywhere, pl.BlockSpec(memory_space=pltpu.VMEM)),
        scratch_shapes=[two] * 2
        + [
            pltpu.VMEM((micro, images, head_count, rows), F32),
            pltpu.VMEM((2, images, rows, depth), BF16),
            pltpu.VMEM((2, 4, 4, rows // 2, depth // 2), BF16),
        ]
        + [blocks] * 4
        + [stats]
        + [blocks] * 5
        + [stats, row, row]
        + [
            pltpu.VMEM((6, 4, total // 8, total // 4), BF16),
            pltpu.VMEM((head_size, total), F32),
            pltpu.VMEM((sections, images, rows, channels), BF16),
            dma((8,)),
            dma(()),
            dma(()),
            dma((2, 20)),
            dma((2, 20)),
            dma((6,)),
            dma((6,)),
            dma((3,)),
            dma((3,)),
            dma((4,)),
            dma(()),
            dma(()),
        ],
        compiler_params=pltpu.CompilerParams(
            collective_id=0, has_side_effects=True, vmem_limit_bytes=62 * 2**20
        ),
        cost_estimate=pl.CostEstimate(
            flops=10 * total * total * head_size, bytes_accessed=32 * total * head_size, transcendentals=0
        ),
        name="attention_backward",
    )(
        plan,
        control_map,
        control_scale,
        saved_q[0],
        saved_k[0],
        saved_v[0],
        saved_o[0],
        saved_lse[0].transpose(0, 1, 3, 2),
        cotangent[0],
        out_weight[0],
    )
    return (dq[None], dk[None], dv[None], control)


def solution(mesh):
    placed = (
        P("section", None, None, "seq", None),
        P("section", None, None, "seq", None),
        P("section", None, None, "seq", None),
        P("section", None, None, "seq", None),
        P("section", None, None, "seq", None),
        P("section", None, "seq", None),
        P("section", "seq", None),
        P("section"),
        P(),
        P(),
    )
    return jax.shard_map(
        shards,
        mesh=mesh,
        in_specs=placed,
        out_specs=(
            P("section", None, "seq", None),
            P("section", None, "seq", None),
            P("section", None, "seq", None),
            P(None, None, "seq", "section"),
        ),
        check_vma=False,
    )
```

time: 214 us -> 171 us (0.80)
  Pallas kernels: 206 us -> 162 us
    pallas_call x1, Pallas kernels: 206 us -> 162 us  [shards(): pl.pallas_call(kernel, out_shape=(rows_out, rows_out, rows_out, jax.Shape...]
where the time goes in v3:
time: 171 us; the launch traced here: 169 us
  Pallas kernels  162 us (95%)
  local copies, waits for them, and re-layouts  5.67 us (3%)
    pallas_call x1, Pallas kernels, shards(): pl.pallas_call(kernel, out_shape=(rows_out, rows_out, rows_out, jax.Shape...  162 us
    unnamed x10, local copies, waits for them, and re-layouts  5.67 us

profile of v3, /device:TPU:0, one launch (start us, length us, event | category | flops | bytes accessed | tf_op | source)
XLA Modules:
  0.0 169.4 jit_solution(15280066644988184161)
XLA Ops:
  1.3 162.4 %attention_backward.1 = (bf16[2,128,2048]{2,1,0:T(8,128)(2,1)}, bf16[2,128,2048]{2,1,0:T(8,128)(2,1)}, bf16[2,128,2048]{2,1,0:T(8,128)(2,1)}, bf16[5,2,128,768]{3,2,1,0:T(8,128)(2,1)}) custom-call(s32[1]{0:T(128)S(6)} %copy.18.plan, s32[5]{0:T(128)} %control_map.1, f32[5]{0:T(128)} %control_scale.1, bf16[2,2,128,2048]{3,2,1,0:T(8,128)(2,1)} %bitcast.15, ...), custom_call_target="tpu_custom_call" | custom-call | flops 21474836480 | bytes 16777216 | tf_op jit(solution)/shard_map/attention_backward/pallas_call | solution.py:474
  163.7 0.0 copy-start.2
  163.7 0.0 copy-start.1
  163.7 2.5 %copy.19 = bf16[1,2,128,2048]{3,2,1,0:T(8,128)(2,1)} copy(bf16[1,2,128,2048]{3,2,1,0:T(8,128)(2,1)} %bitcast.14) | data formatting | bytes 2097152
  166.2 0.0 copy-done.2
  166.2 0.0 copy-start
  166.2 1.0 copy.20
  167.1 0.0 copy-done.1
  167.1 1.0 copy.21
  168.1 0.0 copy-done
  168.1 1.3 copy.22
Async XLA Ops:
  163.7 2.5 %copy-start.2 = (bf16[2,128,2048]{2,1,0:T(8,128)(2,1)S(1)}, bf16[2,128,2048]{2,1,0:T(8,128)(2,1)}, u32[]{:S(2)}) copy-start(bf16[2,128,2048]{2,1,0:T(8,128)(2,1)} %get-tuple-element.9) | copy-start | bytes 3145732
  163.7 3.4 %copy-start.1 = (bf16[2,128,2048]{2,1,0:T(8,128)(2,1)S(1)}, bf16[2,128,2048]{2,1,0:T(8,128)(2,1)}, u32[]{:S(2)}) copy-start(bf16[2,128,2048]{2,1,0:T(8,128)(2,1)} %get-tuple-element.10) | copy-start | bytes 3145732
  166.2 1.9 %copy-start = (bf16[5,2,128,768]{3,2,1,0:T(8,128)(2,1)S(1)}, bf16[5,2,128,768]{3,2,1,0:T(8,128)(2,1)}, u32[]{:S(2)}) copy-start(bf16[5,2,128,768]{3,2,1,0:T(8,128)(2,1)} %get-tuple-element.19) | copy-start | bytes 5898244

commit v4 on v3

--- a/solution.py
+++ b/solution.py
@@ -57,6 +57,7 @@
     delta_row,
     kept,
     dq_sum,
+    dk_sum,
     pieces,
     load_sem,
     swap_s,
@@ -240,8 +241,6 @@
     for p in range(2):
         start_second(p, 1)
         start_second(p, 2)
-    loads[3].wait()
-    select(first_two, v_send, v, 2)
 
     def start_forward(group):
         at = ring_offset(group)
@@ -258,8 +257,6 @@
         first[p][2].wait_recv()
         first[p][3].wait_recv()
         start_second(p, 3)
-    loads[4].wait()
-    select(second_two, o_send, o, 3)
     for group in range(1, 4):
         start_forward(group)
     for group in range(4):
@@ -301,6 +298,12 @@
                     def _():
                         g[0] = g_send[me]
 
+    loads[4].wait()
+    select(second_two, o_send, o, 3)
+
+    loads[3].wait()
+    select(first_two, v_send, v, 2)
+
     channels = pieces.shape[3]
 
     def piece(to):
@@ -313,6 +316,20 @@
     def _(step):
         to = (section + step) % 4
         remote(piece(to), pieces.at[section], piece_s, piece_r, {"section": to}).start()
+
+    total = devices * rows
+    my_image, my_columns = me // heads, columns(me % heads)
+
+    def give_back(send, out, sem, slot):
+        place = out.at[my_image, :, my_columns]
+
+        @pl.when(slot != 0)
+        def _():
+            remote(send.at[slot], place, back_s.at[sem], back_r.at[sem], {"seq": peer(slot)}).start()
+
+        @pl.when(slot == 0)
+        def _():
+            local(send.at[slot], place, own_sem.at[sem]).start()
 
     key_blocks = 4
     query_blocks = 8
@@ -347,11 +364,7 @@
 
         lax.fori_loop(0, devices // query_blocks, keep, 0, unroll=4)
 
-    arrived(v, 2)
-    arrived(o, 3)
     arrived(g, 4)
-    for sem, send in ((1, q_send), (2, v_send), (3, o_send), (4, g_send), (5, stat_send)):
-        sent(send, sem)
 
     low_lane = lane < head_size // 2
     for pair in range(devices // 2):
@@ -363,22 +376,31 @@
         two = jnp.where(straight, pltpu.roll(two, head_size // 2, 1), two)
         for slot, joined in zip(slots, (one, two)):
             g[slot] = joined.astype(BF16)
-            products = joined * o[slot].astype(F32)
-            delta_row[:, slot * rows : (slot + 1) * rows] = jnp.sum(products.T, axis=0, keepdims=True)
-
-    total = devices * rows
-    my_image, my_columns = me // heads, columns(me % heads)
-
-    def give_back(send, out, sem, slot):
-        place = out.at[my_image, :, my_columns]
-
-        @pl.when(slot != 0)
-        def _():
-            remote(send.at[slot], place, back_s.at[sem], back_r.at[sem], {"seq": peer(slot)}).start()
-
-        @pl.when(slot == 0)
-        def _():
-            local(send.at[slot], place, own_sem.at[sem]).start()
+
+    sent(q_send, 1)
+
+    def give_values(u, sum_v):
+        q_send[pl.ds(u * key_blocks, key_blocks)] = sum_v.astype(BF16).reshape(key_blocks, rows, head_size)
+
+        @pl.loop(0, key_blocks)
+        def _(n):
+            give_back(q_send, dv_out, 1, u * key_blocks + n)
+
+    @pl.loop(0, kept.shape[0])
+    def _(u):
+        def inner(t, sum_v):
+            return sum_v + dot(kept[u, t], queries_of(g, t), NN)
+
+        zeros = jnp.zeros((key_rows, head_size), F32)
+        give_values(u, lax.fori_loop(0, devices // query_blocks, inner, zeros, unroll=4))
+
+    arrived(v, 2)
+    arrived(o, 3)
+    for sem, send in ((2, v_send), (3, o_send), (4, g_send), (5, stat_send)):
+        sent(send, sem)
+    for slot in range(devices):
+        products = g[slot].astype(F32) * o[slot].astype(F32)
+        delta_row[:, slot * rows : (slot + 1) * rows] = jnp.sum(products.T, axis=0, keepdims=True)
 
     dq_sum[...] = jnp.zeros_like(dq_sum)
 
@@ -390,39 +412,68 @@
             sum_k, sum_v = carry
             qb, gb = queries_of(q, t), queries_of(g, t)
             if have:
-                rounded = kept[u, t]
-                p = rounded.astype(F32)
+                p = kept[u, t].astype(F32)
             else:
                 p = probabilities(kb, qb, t)
-                rounded = p.astype(BF16)
-            sum_v = sum_v + dot(rounded, gb, NN)
+                sum_v = sum_v + dot(p.astype(BF16), gb, NN)
             ds = (p * (dot(vb, gb, NT) - row_of(delta_row, t))).astype(BF16)
             sum_k = sum_k + dot(ds, qb, NN)
             dq_sum[:, pl.ds(pl.multiple_of(t * query_rows, query_rows), query_rows)] += dot(kt, ds, NN)
             return sum_k, sum_v
 
         zeros = jnp.zeros((key_rows, head_size), F32)
-        sum_k, sum_v = lax.fori_loop(0, devices // query_blocks, inner, (zeros, zeros), unroll=4)
+        sum_k, sum_v = lax.fori_loop(
+            0, devices // query_blocks, inner, (zeros, None if have else zeros), unroll=4
+        )
         slots = pl.ds(u * key_blocks, key_blocks)
         k_send[slots] = (sum_k * scale).astype(BF16).reshape(key_blocks, rows, head_size)
-        v_send[slots] = sum_v.astype(BF16).reshape(key_blocks, rows, head_size)
 
         @pl.loop(0, key_blocks)
         def _(n):
             give_back(k_send, dk_out, 0, u * key_blocks + n)
-            give_back(v_send, dv_out, 1, u * key_blocks + n)
-
-    @pl.loop(0, kept.shape[0])
-    def _(u):
-        key_block(u, True)
+
+        if not have:
+            give_values(u, sum_v)
+
+    early = 3
 
     @pl.loop(kept.shape[0], devices // key_blocks)
     def _(u):
         key_block(u, False)
 
-    for source in range(devices):
-        q_send[source] = (dq_sum[:, source * rows : (source + 1) * rows] * scale).T.astype(BF16)
-        give_back(q_send, dq_out, 2, source)
+    @pl.loop(0, early)
+    def _(u):
+        key_block(u, True)
+
+    late = kept.shape[0] - early
+    dk_sum[...] = jnp.zeros_like(dk_sum)
+
+    @pl.loop(0, devices // query_blocks)
+    def _(t):
+        qb, gb = queries_of(q, t), queries_of(g, t)
+        sum_q = dq_sum[:, pl.ds(pl.multiple_of(t * query_rows, query_rows), query_rows)]
+        for n in range(late):
+            u = early + n
+            kb, vb = keys_of(k, u), keys_of(v, u)
+            p = kept[u, t].astype(F32)
+            ds = (p * (dot(vb, gb, NT) - row_of(delta_row, t))).astype(BF16)
+            dk_sum[n * key_rows : (n + 1) * key_rows, :] += dot(ds, qb, NN)
+            sum_q = sum_q + dot(kb.T, ds, NN)
+        back = (sum_q * scale).T.astype(BF16)
+        v_send[pl.ds(t * query_blocks, query_blocks)] = back.reshape(query_blocks, rows, head_size)
+
+        @pl.loop(0, query_blocks)
+        def _(n):
+            give_back(v_send, dq_out, 2, t * query_blocks + n)
+
+    late_slots = late * key_blocks
+    k_send[pl.ds(early * key_blocks, late_slots)] = (
+        (dk_sum[...] * scale).astype(BF16).reshape(late_slots, rows, head_size)
+    )
+
+    @pl.loop(0, late_slots)
+    def _(n):
+        give_back(k_send, dk_out, 0, early * key_blocks + n)
 
     own_piece.wait()
     three = pl.ds(0, 3)
@@ -436,7 +487,7 @@
     for copies in list(first.values()) + list(second.values()) + list(forward.values()) + [[swap]]:
         for copy in copies:
             copy.wait_send()
-    for sem, (send, out) in enumerate(((k_send, dk_out), (v_send, dv_out), (q_send, dq_out))):
+    for sem, (send, out) in enumerate(((k_send, dk_out), (q_send, dv_out), (v_send, dq_out))):
         local(send.at[some], send.at[some], back_s.at[sem]).wait()
         local(send.at[some], send.at[some], back_r.at[sem]).wait()
         local(send.at[0], out.at[my_image, :, my_columns], own_sem.at[sem]).wait()
@@ -494,6 +545,7 @@
         + [
             pltpu.VMEM((6, 4, total // 8, total // 4), BF16),
             pltpu.VMEM((head_size, total), F32),
+            pltpu.VMEM((total * 3 // 8, head_size), F32),
             pltpu.VMEM((sections, images, rows, channels), BF16),
             dma((8,)),
             dma(()),

time: 171 us -> 164 us (0.959); the launches traced: 169 us -> 164 us
  Pallas kernels: 162 us -> 157 us
    pallas_call x1, Pallas kernels: 162 us -> 157 us  [shards(): pl.pallas_call(kernel, out_shape=(rows_out, rows_out, rows_out, jax.Shape...]
where the time goes in v4:
time: 164 us
  Pallas kernels  157 us (96%)
  local copies, waits for them, and re-layouts  5.67 us (3%)
    pallas_call x1, Pallas kernels, shards(): pl.pallas_call(kernel, out_shape=(rows_out, rows_out, rows_out, jax.Shape...  157 us
    unnamed x10, local copies, waits for them, and re-layouts  5.67 us

profile of v4, /device:TPU:0, one launch (start us, length us, event | category | flops | bytes accessed | tf_op | source)
XLA Modules:
  0.0 164.3 jit_solution(9269653431301140063)
XLA Ops:
  1.3 157.4 %attention_backward.1 = (bf16[2,128,2048]{2,1,0:T(8,128)(2,1)}, bf16[2,128,2048]{2,1,0:T(8,128)(2,1)}, bf16[2,128,2048]{2,1,0:T(8,128)(2,1)}, bf16[5,2,128,768]{3,2,1,0:T(8,128)(2,1)}) custom-call(s32[1]{0:T(128)S(6)} %copy.18.plan, s32[5]{0:T(128)} %control_map.1, f32[5]{0:T(128)} %control_scale.1, bf16[2,2,128,2048]{3,2,1,0:T(8,128)(2,1)} %bitcast.15, ...), custom_call_target="tpu_custom_call" | custom-call | flops 21474836480 | bytes 16777216 | tf_op jit(solution)/shard_map/attention_backward/pallas_call | solution.py:525
  158.6 0.0 copy-start.2
  158.7 0.0 copy-start.1
  158.7 2.5 %copy.19 = bf16[1,2,128,2048]{3,2,1,0:T(8,128)(2,1)} copy(bf16[1,2,128,2048]{3,2,1,0:T(8,128)(2,1)} %bitcast.14) | data formatting | bytes 2097152
  161.1 0.0 copy-done.2
  161.1 0.0 copy-start
  161.1 1.0 copy.20
  162.1 0.0 copy-done.1
  162.1 1.0 copy.21
  163.1 0.0 copy-done
  163.1 1.3 copy.22
Async XLA Ops:
  158.6 2.5 %copy-start.2 = (bf16[2,128,2048]{2,1,0:T(8,128)(2,1)S(1)}, bf16[2,128,2048]{2,1,0:T(8,128)(2,1)}, u32[]{:S(2)}) copy-start(bf16[2,128,2048]{2,1,0:T(8,128)(2,1)} %get-tuple-element.9) | copy-start | bytes 3145732
  158.7 3.4 %copy-start.1 = (bf16[2,128,2048]{2,1,0:T(8,128)(2,1)S(1)}, bf16[2,128,2048]{2,1,0:T(8,128)(2,1)}, u32[]{:S(2)}) copy-start(bf16[2,128,2048]{2,1,0:T(8,128)(2,1)} %get-tuple-element.10) | copy-start | bytes 3145732
  161.1 1.9 %copy-start = (bf16[5,2,128,768]{3,2,1,0:T(8,128)(2,1)S(1)}, bf16[5,2,128,768]{3,2,1,0:T(8,128)(2,1)}, u32[]{:S(2)}) copy-start(bf16[5,2,128,768]{3,2,1,0:T(8,128)(2,1)} %get-tuple-element.19) | copy-start | bytes 5898244

commit v5 on v4

--- a/solution.py
+++ b/solution.py
@@ -178,13 +178,13 @@
         for copy in second[p, group]:
             copy.start()
 
+    swap = remote(cot_in, cot.at[1], swap_s, swap_r, {"seq": index_of(z, y, x + 1)})
+    swap.start()
     for p in range(2):
         src = w_in.at[:, part_columns(p)]
         first[p] = [hop(p, (0, 0), (1, 0), None, 0, src), hop(p, (0, 0), (-1, 0), None, 1, src)]
         for copy in first[p]:
             copy.start()
-    swap = remote(cot_in, cot.at[1], swap_s, swap_r, {"seq": index_of(z, y, x + 1)})
-    swap.start()
     for p in range(2):
         start_second(p, 0)
 

time: 164 us -> 164 us (level)
  no operation moved by 1% of the time
where the time goes in v5:
time: 164 us
  Pallas kernels  157 us (96%)
  local copies, waits for them, and re-layouts  5.67 us (3%)
    pallas_call x1, Pallas kernels, shards(): pl.pallas_call(kernel, out_shape=(rows_out, rows_out, rows_out, jax.Shape...  157 us
    unnamed x10, local copies, waits for them, and re-layouts  5.67 us

profile of v5, /device:TPU:0, one launch (start us, length us, event | category | flops | bytes accessed | tf_op | source)
XLA Modules:
  0.0 164.3 jit_solution(16607668154618661501)
XLA Ops:
  1.3 157.4 %attention_backward.1 = (bf16[2,128,2048]{2,1,0:T(8,128)(2,1)}, bf16[2,128,2048]{2,1,0:T(8,128)(2,1)}, bf16[2,128,2048]{2,1,0:T(8,128)(2,1)}, bf16[5,2,128,768]{3,2,1,0:T(8,128)(2,1)}) custom-call(s32[1]{0:T(128)S(6)} %copy.18.plan, s32[5]{0:T(128)} %control_map.1, f32[5]{0:T(128)} %control_scale.1, bf16[2,2,128,2048]{3,2,1,0:T(8,128)(2,1)} %bitcast.15, ...), custom_call_target="tpu_custom_call" | custom-call | flops 21474836480 | bytes 16777216 | tf_op jit(solution)/shard_map/attention_backward/pallas_call | solution.py:525
  158.6 0.0 copy-start.2
  158.7 0.0 copy-start.1
  158.7 2.5 %copy.19 = bf16[1,2,128,2048]{3,2,1,0:T(8,128)(2,1)} copy(bf16[1,2,128,2048]{3,2,1,0:T(8,128)(2,1)} %bitcast.14) | data formatting | bytes 2097152
  161.1 0.0 copy-done.2
  161.1 0.0 copy-start
  161.1 1.0 copy.20
  162.1 0.0 copy-done.1
  162.1 1.0 copy.21
  163.1 0.0 copy-done
  163.1 1.3 copy.22
Async XLA Ops:
  158.6 2.5 %copy-start.2 = (bf16[2,128,2048]{2,1,0:T(8,128)(2,1)S(1)}, bf16[2,128,2048]{2,1,0:T(8,128)(2,1)}, u32[]{:S(2)}) copy-start(bf16[2,128,2048]{2,1,0:T(8,128)(2,1)} %get-tuple-element.9) | copy-start | bytes 3145732
  158.7 3.4 %copy-start.1 = (bf16[2,128,2048]{2,1,0:T(8,128)(2,1)S(1)}, bf16[2,128,2048]{2,1,0:T(8,128)(2,1)}, u32[]{:S(2)}) copy-start(bf16[2,128,2048]{2,1,0:T(8,128)(2,1)} %get-tuple-element.10) | copy-start | bytes 3145732
  161.1 1.9 %copy-start = (bf16[5,2,128,768]{3,2,1,0:T(8,128)(2,1)S(1)}, bf16[5,2,128,768]{3,2,1,0:T(8,128)(2,1)}, u32[]{:S(2)}) copy-start(bf16[5,2,128,768]{3,2,1,0:T(8,128)(2,1)} %get-tuple-element.19) | copy-start | bytes 5898244
